TPU v7x, 256 devices: a whole 4x4x8 slice. The times are simulated.
256 devices in a mesh: dp: 64 (over y_lo, z, x), tensor: 4 (over y_hi, core).
Axes of the slice: x: 4, y: 4 (y_hi: 2, y_lo: 2; y = y_hi * 2 + y_lo), z: 8, core: 2. Of those that a mesh axis runs over, the one named last changes fastest.
Arguments:
- features: bfloat16 [14336, 12288], P('dp', 'tensor'), may hold values from -6 to 6
- weights: bfloat16 [1536, 96, 128], P(None, 'tensor'), may hold values from -0.109375 to 0.109375
- block_cols: int32 [96, 12], P('tensor'), may hold values from 0 to 47, as said below
- cotangent: bfloat16 [14336, 6144], P('dp', 'tensor'), may hold values from -6 to 6
Outputs:
- input_grad: bfloat16 [14336, 12288], P('dp', 'tensor')
- weight_grad: float32 [1536, 96, 128], P('dp', 'tensor')
Inputs may be any that keep to these rules, and one draw needn't show every extreme that they name: Each row of block_cols names 12 distinct block columns; in each aligned group of four block rows the four rows name disjoint sets, so every block column is named by exactly one row of each group.
All inputs are finite; a program needn't handle non-finite values.
Results may differ from a plain program's by a relative error of at most 0.0049.
Values may be sent and summed in bfloat16 or wider, within the bound.
A program may use at most 192 MiB of HBM per device.

v0:
```python
import jax
import jax.numpy as jnp
from jax import lax
from jax.sharding import PartitionSpec as P

gelu_coef = 0.7978845608


def gelu_slope(pre_act):
    inner_arg = gelu_coef * (pre_act + 0.044715 * pre_act * pre_act * pre_act)
    tanh_val = jnp.tanh(inner_arg)
    return 0.5 * (1.0 + tanh_val) + 0.5 * pre_act * (1.0 - tanh_val * tanh_val) * gelu_coef * (
        1.0 + 0.134145 * pre_act * pre_act
    )


def on_device(features, weights, block_cols, cotangent):
    tok_rows = features.shape[0]
    block_size = weights.shape[2]
    local_rows = weights.shape[1]
    slot_count = block_cols.shape[1]
    col_count = 4 * slot_count
    group_count = local_rows // 4
    blocks = weights.reshape(slot_count, block_size, local_rows, block_size)
    inputs = features.reshape(tok_rows, local_rows, block_size)
    products = jnp.einsum("tri,kirj->trkj", inputs, blocks, preferred_element_type=jnp.float32)
    grouped = products.reshape(tok_rows, group_count, col_count, block_size)
    group_cols = block_cols.reshape(group_count, col_count)
    col_order = jnp.argsort(group_cols, axis=1, stable=True)
    arranged = jnp.take_along_axis(grouped, col_order[None, :, :, None], axis=2)
    partial_sum = jnp.sum(arranged, axis=1).reshape(tok_rows, col_count * block_size)
    full_sum = lax.psum(partial_sum, "tensor")
    upstream = lax.all_gather(cotangent, "tensor", axis=1, tiled=True)
    slope = (upstream.astype(jnp.float32) * gelu_slope(full_sum)).astype(jnp.bfloat16)
    picked = jnp.take(slope.reshape(tok_rows, col_count, block_size), block_cols, axis=1)
    grad_rows = jnp.einsum("trkj,kirj->tri", picked, blocks, preferred_element_type=jnp.float32)
    input_grad = grad_rows.astype(jnp.bfloat16).reshape(tok_rows, local_rows * block_size)
    grad_scale = float(tok_rows * lax.axis_size("dp")) ** (-0.5)
    grad_term = (
        jnp.einsum("tri,trkj->kirj", inputs, picked, preferred_element_type=jnp.float32)
        * grad_scale
    )
    grad_term = grad_term.reshape(slot_count * block_size, local_rows, block_size)
    weight_grad = lax.psum_scatter(grad_term, "dp", scatter_dimension=0, tiled=True)
    return (input_grad, weight_grad)


def solution(mesh):
    return jax.shard_map(
        on_device,
        mesh=mesh,
        in_specs=(P("dp", "tensor"), P(None, "tensor", None), P("tensor", None), P("dp", "tensor")),
        out_specs=(P("dp", "tensor"), P("dp", "tensor", None)),
        check_vma=False,
    )
```

profile of v0, /device:TPU:2, one launch (start us, length us, event | category | flops | bytes accessed | tf_op | source)
XLA Modules:
  0.0 625.0 jit_solution(11741341053819021798)
XLA Ops:
  7.2 0.0 all-gather.2.cloned.1.call-start
  7.2 0.7 all-gather.2.cloned.1.call-update
  7.9 0.0 all-reduce.2.cloned.1.call-start
  7.9 1.6 copy.75
  9.5 0.0 copy-start
  9.5 0.0 copy-start.1
  9.6 18.7 %fusion.5 = f32[24,12,128,224]{2,3,1,0:T(8,128)} fusion(bf16[12,128,24,128]{3,2,1,0:T(8,128)(2,1)} %bitcast.55, bf16[224,24,128,1]{2,1,0,3:T(8,128)(2,1)S(1)} %bitcast.58), kind=kOutput, calls=%fused_computation.10 | convolution fusion | flops 2113929216 | bytes 43843584 | tf_op jit(solution)/shard_map/tri,kirj->trkj/dot_general | solution.py:26
  28.3 0.1 copy.52
  28.4 0.1 reshape.53
  28.4 0.1 copy.53
  28.5 1.0 sort.17
  29.6 0.1 copy.57
  29.6 0.1 reshape.70
  29.7 0.1 copy.54
  29.8 39.2 %gather_fusion.1 = f32[288,224,128]{2,1,0:T(8,128)} fusion(f32[224,6,48,128]{3,0,2,1:T(8,128)} %bitcast.51, s32[288]{0:T(512)S(1)} %reshape.70), kind=kCustom, calls=%fused_computation.1 | custom fusion | bytes 66062592 | tf_op jit(solution)/shard_map/jit(take_along_axis)/gather | solution.py:30
  69.1 13.3 %select_reduce_fusion = f32[48,224,128]{2,1,0:T(8,128)S(1)} fusion(f32[6,48,224,128]{3,2,1,0:T(8,128)} %bitcast.52, pred[6,48]{1,0:T(8,128)(4,1)S(1)} %copy.54), kind=kLoop, calls=%fused_computation.2 | loop fusion | flops 15138816 | bytes 38535456 | tf_op jit(solution)/shard_map/reduce_sum | solution.py:31
  82.3 3.1 copy_bitcast_fusion
  85.4 0.0 all-reduce.2.cloned.1.call-update
  85.5 0.2 reduce-scatter.2.cloned.1.call-start
  85.7 0.1 copy.59
  85.8 0.1 reshape.64
  85.9 0.1 copy.51
  86.0 0.0 all-gather.2.cloned.1.call-done
  86.0 121.9 %all-reduce.2.cloned.1.call-done = f32[224,6144]{1,0:T(8,128)} async-done(((f32[224,6144]{1,0:T(8,128)}), f32[224,6144]{1,0:T(8,128)}) %all-reduce.2.cloned.1.call-update) | async-done | bytes 5505040 | tf_op jit(solution)/shard_map/psum | solution.py:32
  207.9 5.9 copy_bitcast_fusion.1
  213.9 12.9 %gather_fusion = bf16[288,224,128]{2,1,0:T(8,128)(2,1)} fusion(bf16[224,48,128]{2,0,1:T(8,128)(2,1)S(1)} %copy_bitcast_fusion.1, s32[1024]{0:T(1024)S(1)} %pad_clamp_fusion), kind=kCustom, calls=%fused_computation | custom fusion | bytes 33031296 | tf_op jit(solution)/shard_map/jit(_take)/gather | solution.py:35
  226.8 11.9 %broadcast_multiply_fusion = f32[24,12,128,128]{2,3,1,0:T(8,128)} fusion(bf16[24,12,224,128]{3,2,1,0:T(8,128)(2,1)} %bitcast.53, pred[24,12]{1,0:T(8,128)(4,1)S(1)} %copy.51, bf16[224,24,128,1]{2,1,0,3:T(8,128)(2,1)} %bitcast.59), kind=kOutput, calls=%fused_computation.8 | convolution fusion | flops 2126905344 | bytes 36765984 | tf_op jit(solution)/shard_map/tri,trkj->kirj/dot_general | solution.py:40
  238.7 24.8 %copy.64 = f32[1536,24,128]{2,1,0:T(8,128)} copy(f32[1536,24,128]{2,0,1:T(8,128)} %bitcast.57) | data formatting | bytes 37748736 | tf_op jit(solution)/shard_map/reshape | solution.py:43
  263.5 0.0 reduce-scatter.2.cloned.1.call-update
  263.5 11.1 %fusion.23 = bf16[24,28,8,128]{3,2,1,0:T(8,128)(2,1)S(1)} fusion(bf16[12,128,24,128]{3,2,1,0:T(8,128)(2,1)} %bitcast.56, bf16[24,12,224,128]{3,2,1,0:T(8,128)(2,1)} %bitcast.54, pred[24,12]{1,0:T(8,128)(4,1)S(1)} %copy.51), kind=kOutput, calls=%fused_computation.27 | convolution fusion | flops 2122874880 | bytes 27328800 | tf_op jit(solution)/shard_map/trkj,kirj->tri/dot_general | solution.py:36
  274.6 1.5 copy.91
  276.1 342.4 %reduce-scatter.2.cloned.1.call-done = f32[24,24,128]{2,1,0:T(8,128)} async-done(((f32[1536,24,128]{2,1,0:T(8,128)}), f32[24,24,128]{2,1,0:T(8,128)}) %reduce-scatter.2.cloned.1.call-update) | async-done | bytes 294928 | tf_op jit(solution)/shard_map/reduce_scatter | solution.py:44
  (8 shorter events, 0.1 us)
Async XLA Ops:
  7.2 78.9 %all-gather.2.cloned.1.call-start = ((), (), s32[]{:S(2)}) async-start(), calls=%async_computation.1 | async-start | bytes 3440640 | tf_op jit(solution)/shard_map/all_gather | solution.py:33
  7.9 200.0 %all-reduce.2.cloned.1.call-start = ((), (), s32[]{:S(2)}) async-start(), calls=%async_computation.2 | async-start | bytes 11010048 | tf_op jit(solution)/shard_map/psum | solution.py:32
  9.5 18.8 %copy-start = (bf16[28,8,24,128]{3,2,1,0:T(8,128)(2,1)}, bf16[28,8,24,128]{3,2,1,0:T(8,128)(2,1)S(1)}, u32[]{:S(2)}) copy-start(bf16[28,8,24,128]{3,2,1,0:T(8,128)(2,1)S(1)} %copy.75) | copy-start | bytes 4128772
  9.5 18.7 %copy-start.1 = (s32[24,12]{0,1:T(8,128)S(1)}, s32[24,12]{0,1:T(8,128)}, u32[]{:S(2)}) copy-start(s32[24,12]{0,1:T(8,128)} %param.6) | copy-start | bytes 3460
  85.5 533.0 %reduce-scatter.2.cloned.1.call-start = ((), (), s32[]{:S(2)}) async-start(), calls=%async_computation.3 | async-start | bytes 19169280 | tf_op jit(solution)/shard_map/reduce_scatter | solution.py:44
Sparse Core Ops, SparseCore 0:
  9.8 35.8 all-gather.1
  85.6 122.3 all-reduce.1
  263.6 354.8 reduce-scatter.1
where the time goes:
time: 628 us; the launch traced here: 625 us
  waiting for transfers between devices  465 us (74%)
  local copies, waits for them, and re-layouts  83.8 us (13%)
  matrix products  41.8 us (7%)
  other arithmetic  20.2 us (3%)
  between operations  13.8 us (2%)
    reduce_scatter x1, waiting for transfers between devices, on_device(): lax.psum_scatter(grad_term, 'dp', scatter_dimension=0, tiled=True)  342 us
    psum x1, waiting for transfers between devices, on_device(): full_sum = lax.psum(partial_sum, 'tensor')  122 us
    gather x3, local copies, waits for them, and re-layouts, on_device(): arranged = jnp.take_along_axis(grouped, col_order[None, :, :, None], axis=2)  39.4 us
    reshape x1, local copies, waits for them, and re-layouts, on_device(): grad_term.reshape(slot_count * block_size, local_rows, block_size)  24.8 us
    dot_general x1, matrix products, on_device(): jnp.einsum('tri,kirj->trkj', inputs, blocks, preferred_element_type=jnp.f...  18.7 us
    reduce_sum x1, other arithmetic, on_device(): jnp.sum(arranged, axis=1).reshape(tok_rows, col_count * block_size)  13.3 us
    gather x1, local copies, waits for them, and re-layouts, on_device(): jnp.take(slope.reshape(tok_rows, col_count, block_size), block_cols, axis=1)  12.9 us
  transfers between devices with their start and end apart: 3, of which 2 were waited for; matrix products, arithmetic and copies ran while one was open for 14% of the time, Pallas kernels for 0%

commit v1 on v0

v1 whole, which is shorter than its diff:
```python
import functools

import jax
import jax.numpy as jnp
from jax import lax
from jax.experimental import pallas as pl
from jax.experimental.pallas import tpu as pltpu
from jax.sharding import PartitionSpec as P

MESH = pl.DeviceIdType.MESH
F32 = jnp.float32
BF16 = jnp.bfloat16
gelu_coef = 0.7978845608

ORDER = (
    [("W", 2, 0), ("xs", 0, 0), ("xs", 1, 0), ("W", 0, 0), ("zs", 0, 0), ("zs", 1, 0), ("W", 1, 0), ("W", 3, 0), ("D", 3, 0)]
    + [("zt", 0, 0), ("zt", 1, 0), ("zs", 2, 0), ("zs", 3, 0), ("xt", 0, 0), ("xt", 1, 0), ("xs", 2, 0), ("xs", 3, 0), ("D", 3, 0)]
    + [("zt", 0, 1), ("zt", 1, 1), ("D", 3, 0), ("zt", 2, 0), ("zt", 3, 0), ("xt", 0, 1), ("xt", 1, 1), ("us", 0, 0), ("us", 1, 0), ("D", 3, 0)]
    + [("zt", 0, 2), ("zt", 1, 2), ("D", 3, 0), ("ut", 0, 0), ("ut", 1, 0), ("zt", 2, 1), ("zt", 3, 1), ("xt", 2, 0), ("xt", 3, 0), ("D", 3, 0), ("ut", 0, 1), ("ut", 1, 1)]
    + [("zt", 0, 3), ("zt", 1, 3), ("vs", 0, 0), ("vs", 1, 0), ("zt", 2, 2), ("zt", 3, 2), ("D", 3, 0), ("ut", 0, 2), ("ut", 1, 2), ("vt", 0, 0), ("vt", 1, 0), ("xt", 2, 1), ("xt", 3, 1), ("us", 2, 0), ("us", 3, 0), ("D", 3, 0)]
    + [("ut", 0, 3), ("ut", 1, 3), ("ys", 2, 0), ("vt", 0, 1), ("vt", 1, 1), ("ys", 0, 0), ("ut", 2, 0), ("ut", 3, 0), ("zt", 2, 3), ("zt", 3, 3), ("vs", 2, 0), ("vs", 3, 0)]
    + [("ut", 2, 1), ("ut", 3, 1), ("vt", 2, 0), ("vt", 3, 0), ("ut", 2, 2), ("ut", 3, 2), ("vt", 2, 1), ("vt", 3, 1), ("ys", 1, 0), ("ut", 2, 3), ("ut", 3, 3), ("ys", 3, 0)]
    + [("yt", 2, 0), ("yt", 0, 0), ("yt", 1, 0), ("yt", 3, 0)]
)


def gelu_slope(v):
    th = jnp.tanh(gelu_coef * (v + 0.044715 * v * v * v))
    return 0.5 * (1.0 + th) + 0.5 * v * (1.0 - th * th) * gelu_coef * (1.0 + 0.134145 * v * v)


class Ring:
    def __init__(self, n, pos, ahead, back, load, own, send, recv, ssem, rsem):
        self.n, self.pos, self.devs, self.load, self.own = n, pos, (ahead, back), load, own
        self.send, self.recv, self.ssem, self.rsem = send, recv, ssem, rsem
        self.long = n // 2
        self.started = []

    def hops(self, unit, way):
        return self.long if unit % 2 == way else self.n - 1 - self.long

    def slot(self, unit, way, s):
        return s if unit % 2 == way else self.long + s

    def copy(self, unit, way, s):
        if s == 0:
            src = self.send.at[unit, way]
        else:
            src = self.recv.at[unit, self.slot(unit, way, s - 1)]
        k = self.slot(unit, way, s)
        return pltpu.make_async_remote_copy(
            src_ref=src, dst_ref=self.recv.at[unit, k], send_sem=self.ssem.at[unit, k], recv_sem=self.rsem.at[unit, k],
            device_id=self.devs[way], device_id_type=MESH)

    def at(self, shift):
        return lax.rem(self.pos + (shift + 2 * self.n), self.n)

    def go(self, unit, way, s):
        cp = self.copy(unit, way, s)
        cp.start()
        self.started.append(cp)

    def start(self, unit):
        for way in (unit % 2, 1 - unit % 2):
            far = self.hops(unit, way)
            q = self.at(far if way == 0 else -far)

            def body(i, _, way=way, q=q):
                self.send[unit, way, i] = self.load(unit, q, i).astype(BF16)
                return 0

            lax.fori_loop(0, self.send.shape[2], body, 0)
            self.go(unit, way, 0)

    def step(self, unit, s):
        last = True
        for way in (unit % 2, 1 - unit % 2):
            far = self.hops(unit, way)
            if s < far:
                self.copy(unit, way, s).wait_recv()
            if s < far - 1:
                last = False
                q = self.at(far - 1 - s if way == 0 else 1 + s - far)
                k = self.slot(unit, way, s)

                def body(i, _, q=q, k=k):
                    self.recv[unit, k, i] = (self.recv[unit, k, i].astype(F32) + self.load(unit, q, i)).astype(BF16)
                    return 0

                lax.fori_loop(0, self.send.shape[2], body, 0)
                self.go(unit, way, s + 1)
        if last:
            k0 = self.slot(unit, 0, self.hops(unit, 0) - 1)
            k1 = self.slot(unit, 1, self.hops(unit, 1) - 1)

            def total(i, _):
                v = self.load(unit, self.pos, i) + self.recv[unit, k0, i].astype(F32) + self.recv[unit, k1, i].astype(F32)
                self.own(unit, i, v)
                return 0

            lax.fori_loop(0, self.send.shape[2], total, 0)

    def finish(self):
        for cp in self.started:
            cp.wait_send()


def kernel(scale, inv_ref, col_ref, x_ref, w_ref, ct_ref, dx_ref, wg_ref,
           s_a, s_b, s_c, r_a, r_b, r_c, own_pre, slope, x_row, x_t, part, two_z, two_x, done,
           z_send, z_recv, x_send, x_recv, u_send, u_recv, v_send, v_recv, y_send, y_recv,
           fs, fr, zss, zrs, xss, xrs, uss, urs, vss, vrs, yss, yrs):
    d = lax.axis_index("dp")
    t = lax.axis_index("tensor")
    x, z, ylo = lax.rem(d, 4), lax.rem(d // 4, 8), d // 32
    yhi, core = t // 2, lax.rem(t, 2)

    def at(xx, zz, yy):
        return ((yy * 8 + zz) * 4 + xx, t)

    core_dev = (d, yhi * 2 + 1 - core)
    far_dev = (d, (1 - yhi) * 2 + core)
    y_dev = at(x, z, 1 - ylo)
    zp, zm = at(x, lax.rem(z + 1, 8), ylo), at(x, lax.rem(z + 7, 8), ylo)
    xp, xm = at(lax.rem(x + 1, 4), z, ylo), at(lax.rem(x + 3, 4), z, ylo)

    barrier = pltpu.get_barrier_semaphore()
    for dev in (core_dev, far_dev, y_dev, zp, zm, xp, xm):
        pl.semaphore_signal(barrier, inc=1, device_id=dev, device_id_type=MESH)
    pl.semaphore_wait(barrier, 7)

    tok = x_ref.shape[0]
    x_t[...] = jnp.zeros_like(x_t)
    slope[:, tok:, :] = jnp.zeros((48, slope.shape[1] - tok, 128), BF16)

    for r in range(24):
        x_row[r] = x_ref[:, 128 * r:128 * r + 128]

    def pre_col(c):
        acc = None
        for gp in range(3):
            i0, i1 = 96 * gp + c, 96 * gp + 48 + c
            b0, b1 = inv_ref[0, i0], inv_ref[0, i1]
            r0, r1 = inv_ref[1, i0], inv_ref[1, i1]
            lhs = jnp.concatenate([x_row[r0], x_row[r1]], axis=1)
            rhs = jnp.concatenate([w_ref[b0], w_ref[b1]], axis=0)
            term = jnp.dot(lhs, rhs, preferred_element_type=F32)
            acc = term if acc is None else acc + term
        return acc

    q_a, q_b, q_c, q_d = (1 - yhi) * 2 + 1 - core, (1 - yhi) * 2 + core, yhi * 2 + 1 - core, t

    def piece(kind, src, dst, p, dev):
        return pltpu.make_async_remote_copy(
            src_ref=src, dst_ref=dst, send_sem=fs.at[kind, p], recv_sem=fr.at[kind, p], device_id=dev, device_id_type=MESH)

    def copy_a(p):
        return piece(0, s_a.at[pl.ds(4 * p, 4)], r_a.at[pl.ds(4 * p, 4)], p, core_dev)

    def copy_b(p):
        return piece(1, s_b.at[pl.ds(4 * p, 4)], r_b.at[pl.ds(4 * p, 4)], p, far_dev)

    def copy_c(p):
        return piece(2, s_c.at[pl.ds(4 * p, 4)], r_c.at[pl.ds(4 * p, 4)], p, core_dev)

    def slope_copy(kind, quarter, p, dev):
        ref = slope.at[pl.ds(quarter * 12 + 4 * p, 4), pl.ds(0, tok)]
        return piece(kind, ref, ref, p, dev)

    def part_a(p, _):
        def col(j, _):
            s_a[4 * p + j] = pre_col(q_a * 12 + 4 * p + j).astype(BF16)
            return 0

        lax.fori_loop(0, 4, col, 0)
        copy_a(p).start()
        return 0

    def part_b(p, _):
        copy_a(p).wait_recv()

        def col(j, _):
            s_b[4 * p + j] = (pre_col(q_b * 12 + 4 * p + j) + r_a[4 * p + j].astype(F32)).astype(BF16)
            return 0

        lax.fori_loop(0, 4, col, 0)
        copy_b(p).start()
        return 0

    def part_c(p, _):
        def col(j, _):
            s_c[4 * p + j] = pre_col(q_c * 12 + 4 * p + j).astype(BF16)
            return 0

        lax.fori_loop(0, 4, col, 0)
        copy_c(p).start()
        return 0

    def part_d(p, _):
        copy_c(p).wait_recv()

        def col(j, _):
            own_pre[4 * p + j] = pre_col(q_d * 12 + 4 * p + j) + r_c[4 * p + j].astype(F32)
            return 0

        lax.fori_loop(0, 4, col, 0)
        return 0

    lax.fori_loop(0, 3, part_a, 0)
    lax.fori_loop(0, 3, part_b, 0)
    lax.fori_loop(0, 3, part_c, 0)
    lax.fori_loop(0, 3, part_d, 0)

    def turn(r, _):
        x_t[r, :, 0:tok] = x_row[r].T
        return 0

    lax.fori_loop(0, 24, turn, 0)

    def part_s(p, _):
        copy_b(p).wait_recv()

        def col(j, _):
            i = 4 * p + j
            pre = own_pre[i] + r_b[i].astype(F32)
            up = ct_ref[:, pl.ds(pl.multiple_of(i * 128, 128), 128)].astype(F32)
            slope[q_d * 12 + i, 0:tok, :] = (up * gelu_slope(pre)).astype(BF16)
            return 0

        lax.fori_loop(0, 4, col, 0)
        slope_copy(3, q_d, p, far_dev).start()
        slope_copy(4, q_d, p, core_dev).start()
        return 0

    def part_f(p, _):
        slope_copy(3, q_b, p, far_dev).wait_recv()
        slope_copy(5, q_b, p, core_dev).start()
        return 0

    def part_g(p, _):
        slope_copy(4, q_c, p, core_dev).wait_recv()
        slope_copy(5, q_a, p, core_dev).wait_recv()
        return 0

    lax.fori_loop(0, 3, part_s, 0)
    lax.fori_loop(0, 3, part_f, 0)
    lax.fori_loop(0, 3, part_g, 0)

    def weight_rows(r, _):
        xt = x_t[r]
        for kp in range(6):
            c0, c1 = col_ref[r * 12 + 2 * kp], col_ref[r * 12 + 2 * kp + 1]
            rhs = jnp.concatenate([slope[c0], slope[c1]], axis=1)
            g = jnp.dot(xt, rhs, preferred_element_type=F32)
            part[r, pl.ds(256 * kp, 128), :] = g[:, :128]
            part[r, pl.ds(256 * kp + 128, 128), :] = g[:, 128:]
        return 0

    def input_rows(r, _):
        acc = None
        for kp in range(6):
            b = r * 12 + 2 * kp
            c0, c1 = col_ref[b], col_ref[b + 1]
            lhs = jnp.concatenate([slope[c0], slope[c1]], axis=1)[0:tok]
            rhs = jnp.concatenate([w_ref[b], w_ref[b + 1]], axis=1)
            term = lax.dot_general(lhs, rhs, (((1,), (1,)), ((), ())), preferred_element_type=F32)
            acc = term if acc is None else acc + term
        dx_ref[:, pl.ds(pl.multiple_of(r * 128, 128), 128)] = acc.astype(BF16)
        return 0

    def load_z(unit, q, i):
        h, u = unit // 2, unit % 2
        return part[6 * h + i, pl.ds(pl.multiple_of((u * 8 + q) * 96, 96), 96), :]

    def own_z(unit, i, v):
        two_z[unit, i] = v

    def load_x(unit, q, i):
        h, u = unit // 2, unit % 2
        base = pl.multiple_of(u * 768 + q * 24, 24)
        return jnp.concatenate([part[12 + 6 * h + i, pl.ds(base + 96 * k, 24), :] for k in range(8)], axis=0)

    def own_x(unit, i, v):
        two_x[unit, i] = v.reshape(8, 24, 128)

    def load_u(unit, q, i):
        return two_x[unit, :, q].reshape(144, 128)

    def own_u(unit, i, v):
        done[1, unit // 2, unit % 2] = v

    def load_v(unit, q, i):
        return two_z[unit, :, pl.ds(pl.multiple_of(q * 24, 24), 24), :].reshape(144, 128)

    def own_v(unit, i, v):
        done[0, unit // 2, unit % 2] = v

    rings = {
        "z": Ring(8, z, zp, zm, load_z, own_z, z_send, z_recv, zss, zrs),
        "x": Ring(4, x, xp, xm, load_x, own_x, x_send, x_recv, xss, xrs),
        "u": Ring(8, z, zp, zm, load_u, own_u, u_send, u_recv, uss, urs),
        "v": Ring(4, x, xp, xm, load_v, own_v, v_send, v_recv, vss, vrs),
    }

    def y_copy(k):
        return pltpu.make_async_remote_copy(
            src_ref=y_send.at[k], dst_ref=y_recv.at[k], send_sem=yss.at[k], recv_sem=yrs.at[k], device_id=y_dev, device_id_type=MESH)

    row = 0
    for kind, unit, s in ORDER:
        if kind == "W":
            lax.fori_loop(6 * unit, 6 * unit + 6, weight_rows, 0)
        elif kind == "D":
            lax.fori_loop(row, row + unit, input_rows, 0)
            row += unit
        elif kind == "ys":
            y_send[unit] = done[unit // 2, unit % 2, 1 - ylo].astype(BF16)
            y_copy(unit).start()
        elif kind == "yt":
            y_copy(unit).wait_recv()
            v = (done[unit // 2, unit % 2, ylo] + y_recv[unit].astype(F32)) * scale
            wg_ref[pl.ds(6 * unit, 6)] = v.reshape(6, 24, 128)
        elif kind[1] == "s":
            rings[kind[0]].start(unit)
        else:
            rings[kind[0]].step(unit, s)
    assert row == 24

    def drain(p, _):
        copy_a(p).wait_send()
        copy_b(p).wait_send()
        copy_c(p).wait_send()
        slope_copy(3, q_d, p, far_dev).wait_send()
        slope_copy(4, q_d, p, core_dev).wait_send()
        slope_copy(5, q_b, p, core_dev).wait_send()
        return 0

    lax.fori_loop(0, 3, drain, 0)
    for ring in rings.values():
        ring.finish()
    for k in range(4):
        y_copy(k).wait_send()


def on_device(features, weights, block_cols, cotangent):
    tok, width = features.shape
    rows = weights.shape[1]
    w_blocks = weights.reshape(12, 128, rows, 128).transpose(2, 0, 1, 3).reshape(rows * 12, 128, 128)
    flat = block_cols.reshape(rows * 12)
    grouped = block_cols.reshape(rows // 4, 48)
    hit = grouped[:, :, None] == jnp.arange(48, dtype=jnp.int32)[None, None, :]
    block = jnp.arange(rows * 12, dtype=jnp.int32).reshape(rows // 4, 48)
    inv = jnp.stack([
        jnp.sum(jnp.where(hit, block[:, :, None], 0), axis=1).reshape(-1),
        jnp.sum(jnp.where(hit, (block // 12)[:, :, None], 0), axis=1).reshape(-1),
    ])
    scale = float(tok * lax.axis_size("dp")) ** (-0.5)
    vmem = pl.BlockSpec(memory_space=pltpu.VMEM)
    smem = pl.BlockSpec(memory_space=pltpu.SMEM)
    dma = pltpu.SemaphoreType.DMA
    quarter = pltpu.VMEM((12, tok, 128), BF16)
    dx, wg = pl.pallas_call(
        functools.partial(kernel, scale),
        out_shape=(jax.ShapeDtypeStruct((tok, width), BF16), jax.ShapeDtypeStruct((rows, 24, 128), F32)),
        in_specs=[smem, smem, vmem, vmem, vmem],
        out_specs=(vmem, vmem),
        scratch_shapes=[
            quarter, quarter, quarter, quarter, quarter, quarter,
            pltpu.VMEM((12, tok, 128), F32),
            pltpu.VMEM((48, 256, 128), BF16),
            pltpu.VMEM((rows, tok, 128), BF16),
            pltpu.VMEM((rows, 128, 256), BF16),
            pltpu.VMEM((rows, 1536, 128), F32),
            pltpu.VMEM((4, 6, 96, 128), F32),
            pltpu.VMEM((4, 6, 8, 24, 128), F32),
            pltpu.VMEM((2, 2, 2, 144, 128), F32),
            pltpu.VMEM((4, 2, 6, 96, 128), BF16),
            pltpu.VMEM((4, 7, 6, 96, 128), BF16),
            pltpu.VMEM((4, 2, 6, 192, 128), BF16),
            pltpu.VMEM((4, 3, 6, 192, 128), BF16),
            pltpu.VMEM((4, 2, 1, 144, 128), BF16),
            pltpu.VMEM((4, 7, 1, 144, 128), BF16),
            pltpu.VMEM((4, 2, 1, 144, 128), BF16),
            pltpu.VMEM((4, 3, 1, 144, 128), BF16),
            pltpu.VMEM((4, 144, 128), BF16),
            pltpu.VMEM((4, 144, 128), BF16),
            dma((6, 3)), dma((6, 3)),
            dma((4, 7)), dma((4, 7)),
            dma((4, 3)), dma((4, 3)),
            dma((4, 7)), dma((4, 7)),
            dma((4, 3)), dma((4, 3)),
            dma((4,)), dma((4,)),
        ],
        compiler_params=pltpu.CompilerParams(
            collective_id=0, has_side_effects=True, vmem_limit_bytes=63 * 2**20),
        name="block_grads",
    )(inv, flat, features, w_blocks, cotangent)
    return dx, wg.transpose(1, 0, 2)


def solution(mesh):
    return jax.shard_map(
        on_device,
        mesh=mesh,
        in_specs=(P("dp", "tensor"), P(None, "tensor", None), P("tensor", None), P("dp", "tensor")),
        out_specs=(P("dp", "tensor"), P("dp", "tensor", None)),
        check_vma=False,
    )
```

time: 628 us -> 138 us (0.22)
  waiting for transfers between devices: 465 us -> 0 us
  Pallas kernels: 0 us -> 120 us
  local copies, waits for them, and re-layouts: 83.8 us -> 15.8 us
  matrix products: 41.8 us -> 0 us
  other arithmetic: 20.2 us -> 0.8 us
  between operations: 13.8 us -> 0.65 us
    reduce_scatter x1 -> x0, waiting for transfers between devices: 342 us -> none  [on_device(): lax.psum_scatter(grad_term, 'dp', scatter_dimension=0, tiled=True)]
    psum x1 -> x0, waiting for transfers between devices: 122 us -> none  [on_device(): full_sum = lax.psum(partial_sum, 'tensor')]
    pallas_call x0 -> x1, Pallas kernels: none -> 120 us  [on_device(): pl.pallas_call(functools.partial(kernel, scale), out_shape=(jax.ShapeDtyp...]
    gather x4 -> x0, local copies, waits for them, and re-layouts: 52.2 us -> none  [the longest x3 39.4 us: on_device(): arranged = jnp.take_along_axis(grouped, col_order[None, :, :, None], axis=2)]
    dot_general x3 -> x0, matrix products: 41.8 us -> none  [the longest x1 18.7 us: on_device(): jnp.einsum('tri,kirj->trkj', inputs, blocks, preferred_element_type=jnp.f...]
    reshape x5 -> x2, local copies, waits for them, and re-layouts: 29.5 us -> 10.5 us  [the longest x1 9.84 us: on_device(): weights.reshape(12, 128, rows, 128).transpose(2, 0, 1, 3)]
    reduce_sum x1, other arithmetic: 13.3 us -> 0.19 us  [on_device(): jnp.sum(jnp.where(hit, block[:, :, None], 0), axis=1).reshape(-1)]
  transfers between devices with their start and end apart: 3 -> 0, of which waited for: 2 -> 0; matrix products, arithmetic and copies ran while one was open for 14% -> 0% of each run, Pallas kernels for 0% -> 0%
where the time goes in v1:
time: 138 us; the launch traced here: 137 us
  Pallas kernels  120 us (87%)
  local copies, waits for them, and re-layouts  15.8 us (11%)
    pallas_call x1, Pallas kernels, on_device(): pl.pallas_call(functools.partial(kernel, scale), out_shape=(jax.ShapeDtyp...  120 us
    reshape x1, local copies, waits for them, and re-layouts, on_device(): weights.reshape(12, 128, rows, 128).transpose(2, 0, 1, 3)  9.84 us
    unnamed x3, local copies, waits for them, and re-layouts  5.01 us

profile of v1, /device:TPU:2, one launch (start us, length us, event | category | flops | bytes accessed | tf_op | source)
XLA Modules:
  0.0 137.1 jit_solution(13128873920661754205)
XLA Ops:
  0.6 0.8 copy.12
  1.4 0.7 reshape.37.col_ref
  2.1 0.1 eq.15
  2.2 0.2 select_reduce_fusion.1
  2.4 0.1 stack_reshape.6
  2.5 0.1 stack_reshape.7
  2.5 0.6 pad_add_fusion.inv_ref
  3.1 9.8 %copy.14 = bf16[12,128,24,128]{3,1,0,2:T(8,128)(2,1)} copy(bf16[12,128,24,128]{3,2,1,0:T(8,128)(2,1)} %bitcast.6) | data formatting | bytes 18874368 | tf_op jit(solution)/shard_map/reshape | solution.py:347
  13.0 119.9 %block_grads.1 = (bf16[224,3072]{1,0:T(8,128)(2,1)}, f32[24,24,128]{2,1,0:T(8,128)}) custom-call(s32[2,288]{1,0:T(2,128)} %pad_add_fusion.inv_ref, s32[288]{0:T(512)} %reshape.37.col_ref, bf16[224,3072]{1,0:T(8,128)(2,1)} %x_ref.1, bf16[288,128,128]{2,1,0:T(8,128)(2,1)} %bitcast.5, bf16[224,1536]{1,0:T(8,128)(2,1)} %ct_ref.1), custom_call_target="tpu_custom_call" | custom-call | tf_op jit(solution)/shard_map/block_grads/pallas_call | solution.py:361
  132.9 1.7 %copy.15 = f32[24,24,128]{2,1,0:T(8,128)} copy(f32[24,24,128]{2,0,1:T(8,128)} %bitcast.7) | data formatting | bytes 589824
  134.6 2.5 %copy.17 = bf16[224,3072]{1,0:T(8,128)(2,1)} copy(bf16[224,3072]{1,0:T(8,128)(2,1)} %get-tuple-element.18) | data formatting | bytes 2752512
  (1 shorter events, 0.0 us)

commit v2 on v0

v2 whole, which is shorter than its diff:
```python
import functools

import jax
import jax.numpy as jnp
from jax import lax
from jax.experimental import pallas as pl
from jax.experimental.pallas import tpu as pltpu
from jax.sharding import PartitionSpec as P

MESH = pl.DeviceIdType.MESH
F32 = jnp.float32
BF16 = jnp.bfloat16
gelu_coef = 0.7978845608

GROUPS = "zzxX"
ROWS = 3

ORDER = (
    ("W", 1), ("start", 2, 1), ("start", 3, 1), ("W", 3), ("y1s", 3), ("W", 2), ("start", 4, 1), ("start", 5, 1), ("step", 2, 1, 0),
    ("step", 3, 1, 0), ("W", 0), ("start", 0, 1), ("start", 1, 1), ("D", 1), ("step", 2, 1, 1), ("D", 3), ("step", 3, 1, 1), ("D", 3),
    ("step", 0, 1, 0), ("step", 4, 1, 0), ("start", 4, 2), ("step", 1, 1, 0), ("D", 3), ("step", 2, 1, 2), ("D", 3), ("y1t", 3), ("start", 6, 1),
    ("step", 3, 1, 2), ("step", 0, 1, 1), ("step", 5, 1, 0), ("step", 4, 2, 0), ("start", 5, 2), ("D", 1), ("step", 1, 1, 1), ("D", 2),
    ("step", 2, 1, 3), ("step", 3, 1, 3), ("start", 2, 2), ("start", 3, 2), ("D", 3), ("step", 0, 1, 2), ("D", 1), ("step", 4, 2, 1), ("D", 1),
    ("step", 5, 2, 0), ("D", 2), ("step", 6, 1, 0), ("start", 6, 2), ("step", 1, 1, 2), ("step", 2, 2, 0), ("step", 3, 2, 0), ("ys", 1),
    ("step", 0, 1, 3), ("start", 0, 2), ("D", 1), ("step", 4, 2, 2), ("step", 5, 2, 1), ("step", 6, 2, 0), ("xl", 1), ("step", 1, 1, 3),
    ("step", 0, 2, 0), ("start", 1, 2), ("step", 4, 2, 3), ("step", 5, 2, 2), ("step", 6, 2, 1), ("out", 1), ("step", 1, 2, 0), ("ys", 0),
    ("step", 5, 2, 3), ("ys", 2), ("step", 6, 2, 2), ("xl", 0), ("xl", 2), ("step", 6, 2, 3), ("xl", 3), ("out", 0), ("out", 2), ("out", 3),
)

UNITS = [(g, u) for g, a in enumerate(GROUPS) for u in ((None,) if a.isupper() else (0, 1))]


def gelu_slope(v):
    th = jnp.tanh(gelu_coef * (v + 0.044715 * v * v * v))
    return 0.5 * (1.0 + th) + 0.5 * v * (1.0 - th * th) * gelu_coef * (1.0 + 0.134145 * v * v)


class Ring:
    def __init__(self, n, pos, ahead, back, units, load, own, send, recv, ssem, rsem):
        self.n, self.pos, self.devs, self.load, self.own = n, pos, (ahead, back), load, own
        self.send, self.recv, self.ssem, self.rsem = send, recv, ssem, rsem
        self.long = n // 2
        self.index = {unit: i for i, unit in enumerate(units)}
        self.started = []

    def ways(self, unit):
        g, u = UNITS[unit]
        first = (g if u is None else u) % 2
        return ((first, self.long, 0), (1 - first, self.n - 1 - self.long, self.long))

    def go(self, unit, way, slot, s):
        j = self.index[unit]
        src = self.send.at[j, way % self.send.shape[1]] if s == 0 else self.recv.at[j, slot + s - 1]
        cp = pltpu.make_async_remote_copy(
            src_ref=src, dst_ref=self.recv.at[j, slot + s], send_sem=self.ssem.at[j, slot + s], recv_sem=self.rsem.at[j, slot + s],
            device_id=self.devs[way], device_id_type=MESH)
        cp.start()
        self.started.append(cp)

    def arrived(self, unit, way, slot, s):
        j = self.index[unit]
        ref = self.recv.at[j, slot + s]
        pltpu.make_async_remote_copy(
            src_ref=ref, dst_ref=ref, send_sem=self.ssem.at[j, slot + s], recv_sem=self.rsem.at[j, slot + s],
            device_id=self.devs[way], device_id_type=MESH).wait_recv()

    def at(self, shift):
        return lax.rem(self.pos + (shift + 2 * self.n), self.n)

    def start(self, unit):
        j = self.index[unit]
        for way, far, slot in self.ways(unit):
            if far == 0:
                continue
            q = self.at(far if way == 0 else -far)

            def body(i, _, way=way, q=q):
                self.send[j, way % self.send.shape[1], i] = self.load(unit, q, i).astype(BF16)
                return 0

            lax.fori_loop(0, self.send.shape[2], body, 0)
            self.go(unit, way, slot, 0)

    def step(self, unit, s):
        j = self.index[unit]
        for way, far, slot in self.ways(unit):
            if s < far:
                self.arrived(unit, way, slot, s)
            if s < far - 1:
                q = self.at(far - 1 - s if way == 0 else 1 + s - far)

                def body(i, _, q=q, k=slot + s):
                    self.recv[j, k, i] = (self.recv[j, k, i].astype(F32) + self.load(unit, q, i)).astype(BF16)
                    return 0

                lax.fori_loop(0, self.send.shape[2], body, 0)
                self.go(unit, way, slot, s + 1)
        if s == self.long - 1:
            ends = [slot + far - 1 for _, far, slot in self.ways(unit) if far]

            def total(i, _):
                v = self.load(unit, self.pos, i)
                for k in ends:
                    v = v + self.recv[j, k, i].astype(F32)
                self.own(unit, i, v)
                return 0

            lax.fori_loop(0, self.send.shape[2], total, 0)

    def finish(self):
        for cp in self.started:
            cp.wait_send()


def kernel(scale, meta_ref, x_hbm, w_hbm, ct_hbm, dx_ref, wg_ref,
           w_ref, raw, ct_ref, s_a, s_b, s_c, r_a, r_b, r_c, slope, x_row, x_in, x_t, part, two_z, two_x, done, last, wg_rows,
           z_send, z_recv, x_send, x_recv, u_send, u_recv, v_send, v_recv, y_send, y_recv, f_send, f_recv, n_send,
           xl, wl, cl, fs, fr, xis, xir, zss, zrs, xss, xrs, uss, urs, vss, vrs, yss, yrs, fss, frs, nss, nrs):
    d = lax.axis_index("dp")
    t = lax.axis_index("tensor")
    x, z, ylo = lax.rem(d, 4), lax.rem(d // 4, 8), d // 32
    yhi, core = t // 2, lax.rem(t, 2)

    def at(xx, zz, yy):
        return ((yy * 8 + zz) * 4 + xx, t)

    core_dev = (d, yhi * 2 + 1 - core)
    far_dev = (d, (1 - yhi) * 2 + core)
    y_dev = at(x, z, 1 - ylo)
    zp, zm = at(x, lax.rem(z + 1, 8), ylo), at(x, lax.rem(z + 7, 8), ylo)
    xhi, xlo = x // 2, lax.rem(x, 2)
    x_far, x_dev = at(lax.rem(x + 2, 4), z, ylo), at(x + 1 - 2 * xlo, z, ylo)
    base = 12 * xlo

    barrier = pltpu.get_barrier_semaphore()
    for dev in (core_dev, far_dev, y_dev, zp, zm, x_far, x_dev):
        pl.semaphore_signal(barrier, inc=1, device_id=dev, device_id_type=MESH)

    tok = x_hbm.shape[0]

    def x_copy(r):
        return pltpu.make_async_copy(x_hbm.at[:, pl.ds(128 * r, 128)], x_row.at[r], xl.at[r])

    def w_copy(k):
        return pltpu.make_async_copy(w_hbm.at[pl.ds(128 * k, 128)], raw.at[k], wl.at[k])

    ct_copy = pltpu.make_async_copy(ct_hbm, ct_ref, cl)
    for k in range(12):
        w_copy(k).start()
    for r in range(24):
        x_copy(r).start()
    ct_copy.start()
    x_t[...] = jnp.zeros_like(x_t)
    slope[:, tok:256, :] = jnp.zeros((48, 256 - tok, 128), BF16)
    slope[:, 256 + tok:, :] = jnp.zeros((48, 256 - tok, 128), BF16)

    for k in range(12):
        w_copy(k).wait()
        for half in range(2):
            part[half] = raw[k, 64 * half:64 * half + 64].astype(F32).reshape(1536, 128)

            def sort_rows(r, _, k=k, half=half):
                w_ref[r * 12 + k, 64 * half:64 * half + 64, :] = part[half, pl.ds(r, 64, stride=24), :].astype(BF16)
                return 0

            lax.fori_loop(0, 24, sort_rows, 0, unroll=4)
    for r in range(24):
        x_copy(r).wait()

    def pre_col(c):
        acc = None
        for gp in range(3):
            b0, b1 = meta_ref[2 * gp, c], meta_ref[2 * gp + 1, c]
            r0, r1 = lax.div(b0, 12), lax.div(b1, 12)
            lhs = jnp.concatenate([x_row[r0], x_row[r1]], axis=1)
            rhs = jnp.concatenate([w_ref[b0], w_ref[b1]], axis=0)
            term = jnp.dot(lhs, rhs, preferred_element_type=F32)
            acc = term if acc is None else acc + term
        return acc

    q_a, q_b, q_c, q_d = (1 - yhi) * 2 + 1 - core, (1 - yhi) * 2 + core, yhi * 2 + 1 - core, t

    def piece(kind, src, dst, p, dev):
        return pltpu.make_async_remote_copy(
            src_ref=src, dst_ref=dst, send_sem=fs.at[kind, p], recv_sem=fr.at[kind, p], device_id=dev, device_id_type=MESH)

    def copy_a(p):
        return piece(0, s_a.at[pl.ds(2 * p, 2)], r_a.at[pl.ds(2 * p, 2)], p, core_dev)

    def copy_b(p):
        return piece(1, s_b.at[pl.ds(2 * p, 2)], r_b.at[pl.ds(2 * p, 2)], p, far_dev)

    def copy_c(p):
        return piece(2, s_c.at[pl.ds(2 * p, 2)], r_c.at[pl.ds(2 * p, 2)], p, core_dev)

    def slope_copy(kind, quarter, p, dev, src=0, dst=0):
        cols = pl.ds(quarter * 12 + 2 * p, 2)
        return piece(kind, slope.at[cols, pl.ds(src, tok)], slope.at[cols, pl.ds(dst, tok)], p, dev)

    def far_copy(p):
        return slope_copy(3, q_d, p, far_dev)

    def core_copy(i, p):
        return slope_copy((4, 5, 8, 9)[i], q_b if i % 2 else q_d, p, core_dev, i // 2 * 256, i // 2 * 256)

    def x_copy_out(i, p):
        return slope_copy(6 + i, q_b if i else q_d, p, x_dev, 0, 256)

    x_move = pltpu.make_async_remote_copy(
        src_ref=x_row.at[pl.ds(12 - base, 12)], dst_ref=x_in, send_sem=xis, recv_sem=xir, device_id=x_dev, device_id_type=MESH)

    def part_a(p, _):
        for i in (2 * p, 2 * p + 1):
            s_a[i] = pre_col(q_a * 12 + i).astype(BF16)
        copy_a(p).start()
        return 0

    def part_b(p, _):
        copy_a(p).wait_recv()
        for i in (2 * p, 2 * p + 1):
            s_b[i] = (pre_col(q_b * 12 + i) + r_a[i].astype(F32)).astype(BF16)
        copy_b(p).start()
        return 0

    def part_ab(p, _):
        part_a(p + 1, 0)
        return part_b(p, 0)

    def part_c(p, _):
        for i in (2 * p, 2 * p + 1):
            s_c[i] = pre_col(q_c * 12 + i).astype(BF16)
        copy_c(p).start()
        return 0

    def part_d(p, _):
        copy_c(p).wait_recv()
        for i in (2 * p, 2 * p + 1):
            part[p, pl.ds(tok * (i - 2 * p), tok), :] = pre_col(q_d * 12 + i) + r_c[i].astype(F32)
        return 0

    pl.semaphore_wait(barrier, 7)
    x_move.start()
    part_a(0, 0)
    lax.fori_loop(0, 5, part_ab, 0)
    part_b(5, 0)
    lax.fori_loop(0, 6, part_c, 0)
    lax.fori_loop(0, 6, part_d, 0)

    def turn(r, _):
        x_t[r, :, 0:tok] = x_row[base + r].T
        x_t[r, :, 256:256 + tok] = x_in[r].T
        return 0

    def part_s(p, _):
        copy_b(p).wait_recv()
        for i in (2 * p, 2 * p + 1):
            pre = part[p, pl.ds(tok * (i - 2 * p), tok), :] + r_b[i].astype(F32)
            up = ct_ref[:, pl.ds(pl.multiple_of(i * 128, 128), 128)].astype(F32)
            slope[q_d * 12 + i, 0:tok, :] = (up * gelu_slope(pre)).astype(BF16)
        far_copy(p).start()
        core_copy(0, p).start()
        x_copy_out(0, p).start()
        return 0

    def relay(p, _):
        slope_copy(6, q_d, p, x_dev, 256, 256).wait_recv()
        core_copy(2, p).start()
        slope_copy(3, q_b, p, far_dev).wait_recv()
        x_copy_out(1, p).start()
        core_copy(1, p).start()
        return 0

    def relay_last(p, _):
        slope_copy(7, q_b, p, x_dev, 256, 256).wait_recv()
        core_copy(3, p).start()
        return 0

    def relay_both(p, _):
        relay(p, 0)
        return relay_last(p - 2, 0)

    def gathered(p, _):
        slope_copy(4, q_c, p, core_dev).wait_recv()
        slope_copy(5, q_a, p, core_dev).wait_recv()
        slope_copy(8, q_c, p, core_dev, 256, 256).wait_recv()
        slope_copy(9, q_a, p, core_dev, 256, 256).wait_recv()
        return 0

    ct_copy.wait()
    lax.fori_loop(0, 6, part_s, 0)
    x_move.wait_recv()
    lax.fori_loop(0, 12, turn, 0)
    lax.fori_loop(0, 2, relay, 0)
    lax.fori_loop(2, 6, relay_both, 0)
    lax.fori_loop(4, 6, relay_last, 0)
    lax.fori_loop(0, 6, gathered, 0)

    def column(r, slot):
        return meta_ref[6 + lax.div(r, 4), lax.rem(r, 4) * 12 + slot]

    def weight_rows(j, _):
        xt = x_t[j]
        for kp in range(6):
            c0, c1 = column(base + j, 2 * kp), column(base + j, 2 * kp + 1)
            rhs = jnp.concatenate([slope[c0], slope[c1]], axis=1)
            g = jnp.dot(xt, rhs, preferred_element_type=F32)
            part[j, pl.ds(256 * kp, 128), :] = g[:, :128]
            part[j, pl.ds(256 * kp + 128, 128), :] = g[:, 128:]
        return 0

    def input_rows(r, _):
        acc = None
        for kp in range(6):
            b = r * 12 + 2 * kp
            c0, c1 = column(r, 2 * kp), column(r, 2 * kp + 1)
            lhs = jnp.concatenate([slope[c0], slope[c1]], axis=1)[0:tok]
            rhs = jnp.concatenate([w_ref[b], w_ref[b + 1]], axis=1)
            term = lax.dot_general(lhs, rhs, (((1,), (1,)), ((), ())), preferred_element_type=F32)
            acc = term if acc is None else acc + term
        dx_ref[:, pl.ds(pl.multiple_of(r * 128, 128), 128)] = acc.astype(BF16)
        return 0

    z_units = [i for i, (g, _) in enumerate(UNITS) if GROUPS[g] in "zZ"]
    x_units = [i for i, (g, _) in enumerate(UNITS) if GROUPS[g] in "xX"]

    def half(unit):
        u = UNITS[unit][1]
        return ylo if u is None else u

    def load_z(unit, q, i):
        return part[ROWS * UNITS[unit][0] + i, pl.ds(pl.multiple_of(half(unit) * 768 + q * 96, 32), 96), :]

    def own_z(unit, i, v):
        two_z[z_units.index(unit), i] = v

    def load_x(unit, q, i):
        first = pl.multiple_of(half(unit) * 768 + q * 48, 16)
        row = ROWS * UNITS[unit][0] + i
        return jnp.concatenate([part[row, pl.ds(first + 96 * k, 48), :] for k in range(8)], axis=0)

    def own_x(unit, i, v):
        two_x[x_units.index(unit), i] = v.reshape(8, 48, 128)

    def load_u(unit, q, i):
        return two_x[x_units.index(unit), :, q].reshape(ROWS * 48, 128)

    def load_v(unit, q, i):
        return two_z[z_units.index(unit), :, pl.ds(pl.multiple_of(q * 48, 16), 48), :].reshape(ROWS * 48, 128)

    def own_last(unit, i, v):
        done[unit] = v

    stages = [
        {"z": Ring(8, z, zp, zm, z_units, load_z, own_z, z_send, z_recv, zss, zrs),
         "x": Ring(2, xhi, x_far, x_far, x_units, load_x, own_x, x_send, x_recv, xss, xrs)},
        {"x": Ring(8, z, zp, zm, x_units, load_u, own_last, u_send, u_recv, uss, urs),
         "z": Ring(2, xhi, x_far, x_far, z_units, load_v, own_last, v_send, v_recv, vss, vrs)},
    ]

    def y_copy(g):
        return pltpu.make_async_remote_copy(
            src_ref=y_send.at[g], dst_ref=y_recv.at[g], send_sem=yss.at[g], recv_sem=yrs.at[g], device_id=y_dev, device_id_type=MESH)

    firsts = [g for g, a in enumerate(GROUPS) if a.isupper()]

    def first_copy(g):
        i = firsts.index(g)
        return pltpu.make_async_remote_copy(
            src_ref=f_send.at[i], dst_ref=f_recv.at[i], send_sem=fss.at[i], recv_sem=frs.at[i], device_id=y_dev, device_id_type=MESH)

    def next_copy(g, owner):
        return pltpu.make_async_remote_copy(
            src_ref=n_send.at[g], dst_ref=wg_rows.at[pl.ds(12 * owner + ROWS * g, ROWS)], send_sem=nss.at[g], recv_sem=nrs.at[g],
            device_id=x_dev, device_id_type=MESH)

    row = 0
    waits = []
    for kind, *what in ORDER:
        if kind == "D":
            lax.fori_loop(row, row + what[0], input_rows, 0)
            row += what[0]
            continue
        if kind in ("start", "step"):
            unit, stage = what[:2]
            ring = stages[stage - 1][GROUPS[UNITS[unit][0]].lower()]
            if kind == "start":
                ring.start(unit)
            else:
                ring.step(unit, what[2])
            continue
        g = what[0]
        unit = [i for i, u in enumerate(UNITS) if u[0] == g][0]
        if kind == "W":
            lax.fori_loop(ROWS * g, ROWS * g + ROWS, weight_rows, 0)
        elif kind == "y1s":
            def give(i, _, g=g):
                f_send[firsts.index(g), i] = part[ROWS * g + i, pl.ds(pl.multiple_of((1 - ylo) * 768, 768), 768), :].astype(BF16)
                return 0

            lax.fori_loop(0, ROWS, give, 0)
            first_copy(g).start()
            waits.append(first_copy(g))
        elif kind == "y1t":
            first_copy(g).wait_recv()

            def take(i, _, g=g):
                rows = pl.ds(pl.multiple_of(ylo * 768, 768), 768)
                part[ROWS * g + i, rows, :] = part[ROWS * g + i, rows, :] + f_recv[firsts.index(g), i].astype(F32)
                return 0

            lax.fori_loop(0, ROWS, take, 0)
        elif kind == "ys":
            y_send[g] = done[unit + 1 - ylo].astype(BF16)
            y_copy(g).start()
            waits.append(y_copy(g))
        elif kind == "xl":
            if UNITS[unit][1] is None:
                v = done[unit]
            else:
                y_copy(g).wait_recv()
                v = done[unit + ylo] + y_recv[g].astype(F32)
            last[g] = (v * scale).reshape(ROWS, 48, 128)
            wg_rows[pl.ds(base + ROWS * g, ROWS)] = last[g, :, pl.ds(pl.multiple_of(24 * xlo, 8), 24), :]
            n_send[g] = last[g, :, pl.ds(pl.multiple_of(24 - 24 * xlo, 8), 24), :]
            next_copy(g, xlo).start()
            waits.append(next_copy(g, xlo))
        else:
            next_copy(g, 1 - xlo).wait_recv()
    assert row == 24
    for r in range(24):
        wg_ref[:, r, :] = wg_rows[r]

    def drain(p, _):
        copy_a(p).wait_send()
        copy_b(p).wait_send()
        copy_c(p).wait_send()
        far_copy(p).wait_send()
        for i in range(4):
            core_copy(i, p).wait_send()
        for i in range(2):
            x_copy_out(i, p).wait_send()
        return 0

    lax.fori_loop(0, 6, drain, 0)
    x_move.wait_send()
    for stage in stages:
        for ring in stage.values():
            ring.finish()
    for cp in waits:
        cp.wait_send()


def on_device(features, weights, block_cols, cotangent):
    tok, width = features.shape
    rows = weights.shape[1]
    row = jnp.arange(rows, dtype=jnp.int32)[:, None, None, None]
    slot = jnp.arange(12, dtype=jnp.int32)[None, :, None, None]
    line = jnp.arange(12, dtype=jnp.int32)[None, None, :, None]
    place = jnp.arange(48, dtype=jnp.int32)[None, None, None, :]
    cols = block_cols[:, :, None, None]
    hit = (row // 4 == line % 6) & (jnp.where(line < 6, cols, row % 4 * 12 + slot) == place)
    meta = jnp.sum(jnp.where(hit, jnp.where(line < 6, row * 12 + slot, cols), 0), axis=(0, 1))
    scale = float(tok * lax.axis_size("dp")) ** (-0.5)
    vmem = pl.BlockSpec(memory_space=pltpu.VMEM)
    smem = pl.BlockSpec(memory_space=pltpu.SMEM)
    any_ = pl.BlockSpec(memory_space=pl.ANY)
    dma = pltpu.SemaphoreType.DMA
    quarter = pltpu.VMEM((12, tok, 128), BF16)
    n_groups = len(GROUPS)
    nz = sum(GROUPS[g] in "zZ" for g, _ in UNITS)
    nx = len(UNITS) - nz
    ny = max(1, sum(a.isupper() for a in GROUPS))
    dx, wg = pl.pallas_call(
        functools.partial(kernel, scale),
        out_shape=(jax.ShapeDtypeStruct((tok, width), BF16), jax.ShapeDtypeStruct((24, rows, 128), F32)),
        in_specs=[smem, any_, any_, any_],
        out_specs=(vmem, vmem),
        scratch_shapes=[
            pltpu.VMEM((rows * 12, 128, 128), BF16),
            pltpu.VMEM((12, 128, rows, 128), BF16),
            pltpu.VMEM((tok, 1536), BF16),
            quarter, quarter, quarter, quarter, quarter, quarter,
            pltpu.VMEM((48, 512, 128), BF16),
            pltpu.VMEM((rows, tok, 128), BF16),
            pltpu.VMEM((12, tok, 128), BF16),
            pltpu.VMEM((12, 128, 512), BF16),
            pltpu.VMEM((12, 1536, 128), F32),
            pltpu.VMEM((nz, ROWS, 96, 128), F32),
            pltpu.VMEM((nx, ROWS, 8, 48, 128), F32),
            pltpu.VMEM((len(UNITS), ROWS * 48, 128), F32),
            pltpu.VMEM((n_groups, ROWS, 48, 128), F32),
            pltpu.VMEM((rows, 24, 128), F32),
            pltpu.VMEM((nz, 2, ROWS, 96, 128), BF16),
            pltpu.VMEM((nz, 7, ROWS, 96, 128), BF16),
            pltpu.VMEM((nx, 1, ROWS, 384, 128), BF16),
            pltpu.VMEM((nx, 1, ROWS, 384, 128), BF16),
            pltpu.VMEM((nx, 2, 1, ROWS * 48, 128), BF16),
            pltpu.VMEM((nx, 7, 1, ROWS * 48, 128), BF16),
            pltpu.VMEM((nz, 1, 1, ROWS * 48, 128), BF16),
            pltpu.VMEM((nz, 1, 1, ROWS * 48, 128), BF16),
            pltpu.VMEM((n_groups, ROWS * 48, 128), BF16),
            pltpu.VMEM((n_groups, ROWS * 48, 128), BF16),
            pltpu.VMEM((ny, ROWS, 768, 128), BF16),
            pltpu.VMEM((ny, ROWS, 768, 128), BF16),
            pltpu.VMEM((n_groups, ROWS, 24, 128), F32),
            dma((rows,)), dma((12,)), dma(()),
            dma((10, 6)), dma((10, 6)),
            dma(()), dma(()),
            dma((nz, 7)), dma((nz, 7)),
            dma((nx, 1)), dma((nx, 1)),
            dma((nx, 7)), dma((nx, 7)),
            dma((nz, 1)), dma((nz, 1)),
            dma((n_groups,)), dma((n_groups,)),
            dma((ny,)), dma((ny,)),
            dma((n_groups,)), dma((n_groups,)),
        ],
        compiler_params=pltpu.CompilerParams(
            collective_id=0, has_side_effects=True, vmem_limit_bytes=62 * 2**20),
        name="block_grads",
    )(meta, features, weights, cotangent)
    return dx, wg


def solution(mesh):
    return jax.shard_map(
        on_device,
        mesh=mesh,
        in_specs=(P("dp", "tensor"), P(None, "tensor", None), P("tensor", None), P("dp", "tensor")),
        out_specs=(P("dp", "tensor"), P("dp", "tensor", None)),
        check_vma=False,
    )
```

time: 628 us -> 113 us (0.18)
  waiting for transfers between devices: 465 us -> 0 us
  Pallas kernels: 0 us -> 106 us
  local copies, waits for them, and re-layouts: 83.8 us -> 3.27 us
  matrix products: 41.8 us -> 0 us
  other arithmetic: 20.2 us -> 2.94 us
  between operations: 13.8 us -> 0.68 us
    reduce_scatter x1 -> x0, waiting for transfers between devices: 342 us -> none  [on_device(): lax.psum_scatter(grad_term, 'dp', scatter_dimension=0, tiled=True)]
    psum x1 -> x0, waiting for transfers between devices: 122 us -> none  [on_device(): full_sum = lax.psum(partial_sum, 'tensor')]
    pallas_call x0 -> x1, Pallas kernels: none -> 106 us  [on_device(): pl.pallas_call(functools.partial(kernel, scale), out_shape=(jax.ShapeDtyp...]
    gather x4 -> x0, local copies, waits for them, and re-layouts: 52.2 us -> none  [the longest x3 39.4 us: on_device(): arranged = jnp.take_along_axis(grouped, col_order[None, :, :, None], axis=2)]
    dot_general x3 -> x0, matrix products: 41.8 us -> none  [the longest x1 18.7 us: on_device(): jnp.einsum('tri,kirj->trkj', inputs, blocks, preferred_element_type=jnp.f...]
    reshape x5 -> x0, local copies, waits for them, and re-layouts: 29.5 us -> none  [the longest x1 24.8 us: on_device(): grad_term.reshape(slot_count * block_size, local_rows, block_size)]
    reduce_sum x1, other arithmetic: 13.3 us -> 2.05 us  [on_device(): jnp.sum(jnp.where(hit, jnp.where(line < 6, row * 12 + slot, cols), 0), ax...]
  transfers between devices with their start and end apart: 3 -> 0, of which waited for: 2 -> 0; matrix products, arithmetic and copies ran while one was open for 14% -> 0% of each run, Pallas kernels for 0% -> 0%
where the time goes in v2:
time: 113 us
  Pallas kernels  106 us (94%)
  local copies, waits for them, and re-layouts  3.27 us (3%)
  other arithmetic  2.94 us (3%)
    pallas_call x1, Pallas kernels, on_device(): pl.pallas_call(functools.partial(kernel, scale), out_shape=(jax.ShapeDtyp...  106 us
    unnamed x4, local copies, waits for them, and re-layouts  3.27 us

profile of v2, /device:TPU:2, one launch (start us, length us, event | category | flops | bytes accessed | tf_op | source)
XLA Modules:
  0.0 112.9 jit_solution(17027135065469465506)
XLA Ops:
  0.7 0.1 broadcast_compare_fusion
  0.8 0.8 broadcast_select_fusion.1
  1.6 2.1 %select_reduce_fusion.meta_ref = s32[12,48]{1,0:T(8,128)} fusion(s32[24,12,12]{0,2,1:T(8,128)S(1)} %get-tuple-element.3, s32[24,12,12]{0,2,1:T(8,128)S(1)} %get-tuple-element.2, pred[24,12]{0,1:T(8,128)(4,1)S(1)} %broadcast_compare_fusion), kind=kLoop, calls=%fused_computation | loop fusion | flops 662976 | bytes 30240 | tf_op jit(solution)/shard_map/reduce_sum | solution.py:462
  3.6 106.0 %block_grads.1 = (bf16[224,3072]{1,0:T(8,128)(2,1)}, f32[24,24,128]{2,1,0:T(8,128)}) custom-call(s32[12,48]{1,0:T(8,128)} %select_reduce_fusion.meta_ref, bf16[224,3072]{1,0:T(8,128)(2,1)} %x_hbm.1, bf16[1536,24,128]{2,1,0:T(8,128)(2,1)} %w_hbm.1, bf16[224,1536]{1,0:T(8,128)(2,1)} %ct_hbm.1), custom_call_target="tpu_custom_call" | custom-call | tf_op jit(solution)/shard_map/block_grads/pallas_call | solution.py:473
  109.6 0.0 copy-start
  109.6 2.5 %copy.9 = bf16[224,3072]{1,0:T(8,128)(2,1)} copy(bf16[224,3072]{1,0:T(8,128)(2,1)} %get-tuple-element.8) | data formatting | bytes 2752512
  112.2 0.0 copy-done
  112.2 0.7 copy.10
  (6 shorter events, 0.0 us)
Async XLA Ops:
  109.6 2.6 %copy-start = (f32[24,24,128]{2,1,0:T(8,128)S(1)}, f32[24,24,128]{2,1,0:T(8,128)}, u32[]{:S(2)}) copy-start(f32[24,24,128]{2,1,0:T(8,128)} %get-tuple-element.9) | copy-start | bytes 884740

commit v3 on v2

--- a/solution.py
+++ b/solution.py
@@ -12,19 +12,24 @@
 BF16 = jnp.bfloat16
 gelu_coef = 0.7978845608
 
-GROUPS = "zzxX"
-ROWS = 3
+GROUPS = "zzxxXZ"
+ROWS = 2
+COLS = 3
+PIECES = 12 // COLS
+VIA_X = 3
 
 ORDER = (
-    ("W", 1), ("start", 2, 1), ("start", 3, 1), ("W", 3), ("y1s", 3), ("W", 2), ("start", 4, 1), ("start", 5, 1), ("step", 2, 1, 0),
-    ("step", 3, 1, 0), ("W", 0), ("start", 0, 1), ("start", 1, 1), ("D", 1), ("step", 2, 1, 1), ("D", 3), ("step", 3, 1, 1), ("D", 3),
-    ("step", 0, 1, 0), ("step", 4, 1, 0), ("start", 4, 2), ("step", 1, 1, 0), ("D", 3), ("step", 2, 1, 2), ("D", 3), ("y1t", 3), ("start", 6, 1),
-    ("step", 3, 1, 2), ("step", 0, 1, 1), ("step", 5, 1, 0), ("step", 4, 2, 0), ("start", 5, 2), ("D", 1), ("step", 1, 1, 1), ("D", 2),
-    ("step", 2, 1, 3), ("step", 3, 1, 3), ("start", 2, 2), ("start", 3, 2), ("D", 3), ("step", 0, 1, 2), ("D", 1), ("step", 4, 2, 1), ("D", 1),
-    ("step", 5, 2, 0), ("D", 2), ("step", 6, 1, 0), ("start", 6, 2), ("step", 1, 1, 2), ("step", 2, 2, 0), ("step", 3, 2, 0), ("ys", 1),
-    ("step", 0, 1, 3), ("start", 0, 2), ("D", 1), ("step", 4, 2, 2), ("step", 5, 2, 1), ("step", 6, 2, 0), ("xl", 1), ("step", 1, 1, 3),
-    ("step", 0, 2, 0), ("start", 1, 2), ("step", 4, 2, 3), ("step", 5, 2, 2), ("step", 6, 2, 1), ("out", 1), ("step", 1, 2, 0), ("ys", 0),
-    ("step", 5, 2, 3), ("ys", 2), ("step", 6, 2, 2), ("xl", 0), ("xl", 2), ("step", 6, 2, 3), ("xl", 3), ("out", 0), ("out", 2), ("out", 3),
+    ("W", 3), ("start", 7, 1), ("W", 4), ("y1s", 4), ("start", 6, 1), ("W", 0), ("start", 1, 1), ("start", 0, 1), ("W", 1), ("start", 3, 1),
+    ("start", 2, 1), ("W", 2), ("start", 5, 1), ("W", 5), ("y1s", 5), ("step", 1, 1, 0), ("step", 7, 1, 0), ("start", 7, 2), ("D", 1),
+    ("step", 0, 1, 0), ("D", 2), ("step", 3, 1, 0), ("D", 1), ("start", 4, 1), ("D", 1), ("step", 2, 1, 0), ("D", 3), ("step", 1, 1, 1), ("D", 1),
+    ("step", 6, 1, 0), ("step", 7, 2, 0), ("start", 6, 2), ("D", 2), ("step", 0, 1, 1), ("y1t", 4), ("D", 1), ("start", 8, 1), ("D", 1),
+    ("step", 3, 1, 1), ("D", 2), ("step", 2, 1, 1), ("D", 3), ("step", 5, 1, 0), ("step", 1, 1, 2), ("start", 5, 2), ("D", 1), ("step", 7, 2, 1),
+    ("D", 1), ("step", 6, 2, 0), ("D", 2), ("step", 0, 1, 2), ("D", 2), ("step", 3, 1, 2), ("step", 4, 1, 0), ("start", 4, 2), ("step", 2, 1, 2),
+    ("step", 1, 1, 3), ("y1t", 5), ("start", 9, 1), ("step", 5, 2, 0), ("step", 7, 2, 2), ("step", 6, 2, 1), ("step", 0, 1, 3), ("fs", 0),
+    ("step", 3, 1, 3), ("step", 8, 1, 0), ("start", 8, 2), ("step", 4, 2, 0), ("step", 2, 1, 3), ("fs", 1), ("step", 9, 1, 0), ("step", 5, 2, 1),
+    ("step", 7, 2, 3), ("step", 6, 2, 2), ("ft", 0), ("step", 8, 2, 0), ("step", 4, 2, 1), ("step", 9, 1, 1), ("ft", 1), ("step", 5, 2, 2),
+    ("step", 6, 2, 3), ("fs", 3), ("step", 8, 2, 1), ("step", 4, 2, 2), ("step", 9, 1, 2), ("step", 5, 2, 3), ("step", 8, 2, 2), ("ft", 3),
+    ("step", 4, 2, 3), ("fs", 2), ("step", 9, 1, 3), ("fs", 5), ("step", 8, 2, 3), ("fs", 4), ("ft", 2), ("ft", 5), ("ft", 4),
 )
 
 UNITS = [(g, u) for g, a in enumerate(GROUPS) for u in ((None,) if a.isupper() else (0, 1))]
@@ -112,10 +117,10 @@
             cp.wait_send()
 
 
-def kernel(scale, meta_ref, x_hbm, w_hbm, ct_hbm, dx_ref, wg_ref,
-           w_ref, raw, ct_ref, s_a, s_b, s_c, r_a, r_b, r_c, slope, x_row, x_in, x_t, part, two_z, two_x, done, last, wg_rows,
-           z_send, z_recv, x_send, x_recv, u_send, u_recv, v_send, v_recv, y_send, y_recv, f_send, f_recv, n_send,
-           xl, wl, cl, fs, fr, xis, xir, zss, zrs, xss, xrs, uss, urs, vss, vrs, yss, yrs, fss, frs, nss, nrs):
+def kernel(scale, meta_ref, x_hbm, w_hbm, ct_hbm, dx_hbm, wg_ref,
+           w_ref, raw, ct_ref, dx_ref, s_a, s_b, s_c, r_a, r_b, r_c, slope, slope_next, x_row, x_in, x_t, part, two_z, two_x, done, wg_rows,
+           z_send, z_recv, x_send, x_recv, u_send, u_recv, f_send, f_recv, g_send, g_recv,
+           xl, wl, cl, dl, fs, fr, xis, xir, zss, zrs, xss, xrs, uss, urs, fss, frs, gss, grs):
     d = lax.axis_index("dp")
     t = lax.axis_index("tensor")
     x, z, ylo = lax.rem(d, 4), lax.rem(d // 4, 8), d // 32
@@ -129,11 +134,13 @@
     y_dev = at(x, z, 1 - ylo)
     zp, zm = at(x, lax.rem(z + 1, 8), ylo), at(x, lax.rem(z + 7, 8), ylo)
     xhi, xlo = x // 2, lax.rem(x, 2)
-    x_far, x_dev = at(lax.rem(x + 2, 4), z, ylo), at(x + 1 - 2 * xlo, z, ylo)
+    near = {(dx, dy): at(lax.rem(x + dx, 4), z, lax.rem(ylo + dy, 2)) for dx in range(4) for dy in range(2) if dx or dy}
+    x_far, x_dev = near[2, 0], at(x + 1 - 2 * xlo, z, ylo)
+    pair = {(0, 1): y_dev, (1, 0): x_dev, (1, 1): at(x + 1 - 2 * xlo, z, 1 - ylo)}
     base = 12 * xlo
 
     barrier = pltpu.get_barrier_semaphore()
-    for dev in (core_dev, far_dev, y_dev, zp, zm, x_far, x_dev):
+    for dev in (core_dev, far_dev, zp, zm, *near.values()):
         pl.semaphore_signal(barrier, inc=1, device_id=dev, device_id_type=MESH)
 
     tok = x_hbm.shape[0]
@@ -145,15 +152,21 @@
         return pltpu.make_async_copy(w_hbm.at[pl.ds(128 * k, 128)], raw.at[k], wl.at[k])
 
     ct_copy = pltpu.make_async_copy(ct_hbm, ct_ref, cl)
+    for r in range(24):
+        x_copy(r).start()
     for k in range(12):
         w_copy(k).start()
-    for r in range(24):
-        x_copy(r).start()
     ct_copy.start()
     x_t[...] = jnp.zeros_like(x_t)
-    slope[:, tok:256, :] = jnp.zeros((48, 256 - tok, 128), BF16)
-    slope[:, 256 + tok:, :] = jnp.zeros((48, 256 - tok, 128), BF16)
-
+    slope[:, tok:, :] = jnp.zeros((48, 256 - tok, 128), BF16)
+    slope_next[:, tok:, :] = jnp.zeros((48, 256 - tok, 128), BF16)
+
+    for r in range(24):
+        x_copy(r).wait()
+    x_move = pltpu.make_async_remote_copy(
+        src_ref=x_row.at[pl.ds(12 - base, 12)], dst_ref=x_in, send_sem=xis, recv_sem=xir, device_id=x_dev, device_id_type=MESH)
+    pl.semaphore_wait(barrier, 11)
+    x_move.start()
     for k in range(12):
         w_copy(k).wait()
         for half in range(2):
@@ -164,13 +177,11 @@
                 return 0
 
             lax.fori_loop(0, 24, sort_rows, 0, unroll=4)
-    for r in range(24):
-        x_copy(r).wait()
 
     def pre_col(c):
         acc = None
         for gp in range(3):
-            b0, b1 = meta_ref[2 * gp, c], meta_ref[2 * gp + 1, c]
+            b0, b1 = meta_ref[96 * gp + c], meta_ref[96 * gp + 48 + c]
             r0, r1 = lax.div(b0, 12), lax.div(b1, 12)
             lhs = jnp.concatenate([x_row[r0], x_row[r1]], axis=1)
             rhs = jnp.concatenate([w_ref[b0], w_ref[b1]], axis=0)
@@ -185,17 +196,18 @@
             src_ref=src, dst_ref=dst, send_sem=fs.at[kind, p], recv_sem=fr.at[kind, p], device_id=dev, device_id_type=MESH)
 
     def copy_a(p):
-        return piece(0, s_a.at[pl.ds(2 * p, 2)], r_a.at[pl.ds(2 * p, 2)], p, core_dev)
+        return piece(0, s_a.at[pl.ds(COLS * p, COLS)], r_a.at[pl.ds(COLS * p, COLS)], p, core_dev)
 
     def copy_b(p):
-        return piece(1, s_b.at[pl.ds(2 * p, 2)], r_b.at[pl.ds(2 * p, 2)], p, far_dev)
+        return piece(1, s_b.at[pl.ds(COLS * p, COLS)], r_b.at[pl.ds(COLS * p, COLS)], p, far_dev)
 
     def copy_c(p):
-        return piece(2, s_c.at[pl.ds(2 * p, 2)], r_c.at[pl.ds(2 * p, 2)], p, core_dev)
+        return piece(2, s_c.at[pl.ds(COLS * p, COLS)], r_c.at[pl.ds(COLS * p, COLS)], p, core_dev)
 
     def slope_copy(kind, quarter, p, dev, src=0, dst=0):
-        cols = pl.ds(quarter * 12 + 2 * p, 2)
-        return piece(kind, slope.at[cols, pl.ds(src, tok)], slope.at[cols, pl.ds(dst, tok)], p, dev)
+        cols = pl.ds(quarter * 12 + COLS * p, COLS)
+        held = {0: slope, 256: slope_next}
+        return piece(kind, held[src].at[cols, pl.ds(0, tok)], held[dst].at[cols, pl.ds(0, tok)], p, dev)
 
     def far_copy(p):
         return slope_copy(3, q_d, p, far_dev)
@@ -206,18 +218,15 @@
     def x_copy_out(i, p):
         return slope_copy(6 + i, q_b if i else q_d, p, x_dev, 0, 256)
 
-    x_move = pltpu.make_async_remote_copy(
-        src_ref=x_row.at[pl.ds(12 - base, 12)], dst_ref=x_in, send_sem=xis, recv_sem=xir, device_id=x_dev, device_id_type=MESH)
-
     def part_a(p, _):
-        for i in (2 * p, 2 * p + 1):
+        for i in [COLS * p + k for k in range(COLS)]:
             s_a[i] = pre_col(q_a * 12 + i).astype(BF16)
         copy_a(p).start()
         return 0
 
     def part_b(p, _):
         copy_a(p).wait_recv()
-        for i in (2 * p, 2 * p + 1):
+        for i in [COLS * p + k for k in range(COLS)]:
             s_b[i] = (pre_col(q_b * 12 + i) + r_a[i].astype(F32)).astype(BF16)
         copy_b(p).start()
         return 0
@@ -227,24 +236,22 @@
         return part_b(p, 0)
 
     def part_c(p, _):
-        for i in (2 * p, 2 * p + 1):
+        for i in [COLS * p + k for k in range(COLS)]:
             s_c[i] = pre_col(q_c * 12 + i).astype(BF16)
         copy_c(p).start()
         return 0
 
     def part_d(p, _):
         copy_c(p).wait_recv()
-        for i in (2 * p, 2 * p + 1):
-            part[p, pl.ds(tok * (i - 2 * p), tok), :] = pre_col(q_d * 12 + i) + r_c[i].astype(F32)
-        return 0
-
-    pl.semaphore_wait(barrier, 7)
-    x_move.start()
+        for i in [COLS * p + k for k in range(COLS)]:
+            part[p, pl.ds(tok * (i - COLS * p), tok), :] = pre_col(q_d * 12 + i) + r_c[i].astype(F32)
+        return 0
+
     part_a(0, 0)
-    lax.fori_loop(0, 5, part_ab, 0)
-    part_b(5, 0)
-    lax.fori_loop(0, 6, part_c, 0)
-    lax.fori_loop(0, 6, part_d, 0)
+    lax.fori_loop(0, PIECES - 1, part_ab, 0)
+    part_b(PIECES - 1, 0)
+    lax.fori_loop(0, PIECES, part_c, 0)
+    lax.fori_loop(0, PIECES, part_d, 0)
 
     def turn(r, _):
         x_t[r, :, 0:tok] = x_row[base + r].T
@@ -253,14 +260,17 @@
 
     def part_s(p, _):
         copy_b(p).wait_recv()
-        for i in (2 * p, 2 * p + 1):
-            pre = part[p, pl.ds(tok * (i - 2 * p), tok), :] + r_b[i].astype(F32)
+        for i in [COLS * p + k for k in range(COLS)]:
+            pre = part[p, pl.ds(tok * (i - COLS * p), tok), :] + r_b[i].astype(F32)
             up = ct_ref[:, pl.ds(pl.multiple_of(i * 128, 128), 128)].astype(F32)
             slope[q_d * 12 + i, 0:tok, :] = (up * gelu_slope(pre)).astype(BF16)
         far_copy(p).start()
         core_copy(0, p).start()
         x_copy_out(0, p).start()
         return 0
+
+    def turn_copy(p):
+        return slope_copy(7, q_d, p, far_dev, 256, 256)
 
     def relay(p, _):
         slope_copy(6, q_d, p, x_dev, 256, 256).wait_recv()
@@ -270,43 +280,66 @@
         core_copy(1, p).start()
         return 0
 
+    def relay_far(p, _):
+        slope_copy(6, q_d, p, x_dev, 256, 256).wait_recv()
+        turn_copy(p).start()
+        core_copy(2, p).start()
+        return 0
+
+    def relay_near(p, _):
+        slope_copy(3, q_b, p, far_dev).wait_recv()
+        core_copy(1, p).start()
+        return 0
+
     def relay_last(p, _):
         slope_copy(7, q_b, p, x_dev, 256, 256).wait_recv()
         core_copy(3, p).start()
         return 0
 
-    def relay_both(p, _):
-        relay(p, 0)
-        return relay_last(p - 2, 0)
-
-    def gathered(p, _):
+    def gathered_own(p, _):
         slope_copy(4, q_c, p, core_dev).wait_recv()
         slope_copy(5, q_a, p, core_dev).wait_recv()
+        return 0
+
+    def gathered(p, _):
         slope_copy(8, q_c, p, core_dev, 256, 256).wait_recv()
         slope_copy(9, q_a, p, core_dev, 256, 256).wait_recv()
         return 0
 
+    def column(r, slot):
+        return meta_ref[288 + r * 12 + slot]
+
+    def weight_part(j, first):
+        xt = x_t[j, :, first:first + 256]
+        slopes = slope_next if first else slope
+        for kp in range(6):
+            c0, c1 = column(base + j, 2 * kp), column(base + j, 2 * kp + 1)
+            rhs = jnp.concatenate([slopes[c0], slopes[c1]], axis=1)
+            g = jnp.dot(xt, rhs, preferred_element_type=F32)
+            for half in range(2):
+                rows = pl.ds(256 * kp + 128 * half, 128)
+                v = g[:, 128 * half:128 * half + 128]
+                part[j, rows, :] = v if first == 0 else part[j, rows, :] + v
+        return 0
+
+    def relay_and_own(p, _):
+        for k in range(COLS):
+            weight_part(COLS * p + k, 0)
+        return relay_last(p, 0)
+
+    def weight_rows(j, _):
+        return weight_part(j, 256)
+
     ct_copy.wait()
-    lax.fori_loop(0, 6, part_s, 0)
+    lax.fori_loop(0, PIECES, part_s, 0)
     x_move.wait_recv()
     lax.fori_loop(0, 12, turn, 0)
-    lax.fori_loop(0, 2, relay, 0)
-    lax.fori_loop(2, 6, relay_both, 0)
-    lax.fori_loop(4, 6, relay_last, 0)
-    lax.fori_loop(0, 6, gathered, 0)
-
-    def column(r, slot):
-        return meta_ref[6 + lax.div(r, 4), lax.rem(r, 4) * 12 + slot]
-
-    def weight_rows(j, _):
-        xt = x_t[j]
-        for kp in range(6):
-            c0, c1 = column(base + j, 2 * kp), column(base + j, 2 * kp + 1)
-            rhs = jnp.concatenate([slope[c0], slope[c1]], axis=1)
-            g = jnp.dot(xt, rhs, preferred_element_type=F32)
-            part[j, pl.ds(256 * kp, 128), :] = g[:, :128]
-            part[j, pl.ds(256 * kp + 128, 128), :] = g[:, 128:]
-        return 0
+    lax.fori_loop(0, VIA_X, relay, 0)
+    lax.fori_loop(VIA_X, PIECES, relay_far, 0)
+    lax.fori_loop(VIA_X, PIECES, relay_near, 0)
+    lax.fori_loop(0, PIECES, gathered_own, 0)
+    lax.fori_loop(0, PIECES, relay_and_own, 0)
+    lax.fori_loop(0, PIECES, gathered, 0)
 
     def input_rows(r, _):
         acc = None
@@ -344,22 +377,14 @@
     def load_u(unit, q, i):
         return two_x[x_units.index(unit), :, q].reshape(ROWS * 48, 128)
 
-    def load_v(unit, q, i):
-        return two_z[z_units.index(unit), :, pl.ds(pl.multiple_of(q * 48, 16), 48), :].reshape(ROWS * 48, 128)
-
     def own_last(unit, i, v):
-        done[unit] = v
+        done[x_units.index(unit)] = v.reshape(ROWS, 48, 128)
 
     stages = [
         {"z": Ring(8, z, zp, zm, z_units, load_z, own_z, z_send, z_recv, zss, zrs),
          "x": Ring(2, xhi, x_far, x_far, x_units, load_x, own_x, x_send, x_recv, xss, xrs)},
-        {"x": Ring(8, z, zp, zm, x_units, load_u, own_last, u_send, u_recv, uss, urs),
-         "z": Ring(2, xhi, x_far, x_far, z_units, load_v, own_last, v_send, v_recv, vss, vrs)},
+        {"x": Ring(8, z, zp, zm, x_units, load_u, own_last, u_send, u_recv, uss, urs)},
     ]
-
-    def y_copy(g):
-        return pltpu.make_async_remote_copy(
-            src_ref=y_send.at[g], dst_ref=y_recv.at[g], send_sem=yss.at[g], recv_sem=yrs.at[g], device_id=y_dev, device_id_type=MESH)
 
     firsts = [g for g, a in enumerate(GROUPS) if a.isupper()]
 
@@ -368,17 +393,32 @@
         return pltpu.make_async_remote_copy(
             src_ref=f_send.at[i], dst_ref=f_recv.at[i], send_sem=fss.at[i], recv_sem=frs.at[i], device_id=y_dev, device_id_type=MESH)
 
-    def next_copy(g, owner):
+    def spread(g):
+        unit = [i for i, u in enumerate(UNITS) if u[0] == g][0]
+        in_z = unit in z_units
+        sums = two_z if in_z else done
+        index = (z_units if in_z else x_units).index(unit)
+        for dx in range(4 if in_z else 2):
+            for dy in range(1 if UNITS[unit][1] is None else 2):
+                i = index if UNITS[unit][1] is None else index + lax.rem(ylo + dy, 2)
+                q = lax.rem(x + dx, 4) if in_z else lax.rem(xlo + dx, 2)
+                dev = (near if in_z else pair).get((dx, dy))
+                yield dx, dy, dev, lambda i=i, q=q: sums[i, :, pl.ds(pl.multiple_of(24 * q, 8), 24), :]
+
+    def give_copy(g, slot, dev):
         return pltpu.make_async_remote_copy(
-            src_ref=n_send.at[g], dst_ref=wg_rows.at[pl.ds(12 * owner + ROWS * g, ROWS)], send_sem=nss.at[g], recv_sem=nrs.at[g],
-            device_id=x_dev, device_id_type=MESH)
-
+            src_ref=g_send.at[g, slot], dst_ref=g_recv.at[g, slot], send_sem=gss.at[g, slot], recv_sem=grs.at[g, slot],
+            device_id=dev, device_id_type=MESH)
+
+    dx_copy = pltpu.make_async_copy(dx_ref, dx_hbm, dl)
     row = 0
     waits = []
     for kind, *what in ORDER:
         if kind == "D":
             lax.fori_loop(row, row + what[0], input_rows, 0)
             row += what[0]
+            if row == 24:
+                dx_copy.start()
             continue
         if kind in ("start", "step"):
             unit, stage = what[:2]
@@ -409,23 +449,23 @@
                 return 0
 
             lax.fori_loop(0, ROWS, take, 0)
-        elif kind == "ys":
-            y_send[g] = done[unit + 1 - ylo].astype(BF16)
-            y_copy(g).start()
-            waits.append(y_copy(g))
-        elif kind == "xl":
-            if UNITS[unit][1] is None:
-                v = done[unit]
-            else:
-                y_copy(g).wait_recv()
-                v = done[unit + ylo] + y_recv[g].astype(F32)
-            last[g] = (v * scale).reshape(ROWS, 48, 128)
-            wg_rows[pl.ds(base + ROWS * g, ROWS)] = last[g, :, pl.ds(pl.multiple_of(24 * xlo, 8), 24), :]
-            n_send[g] = last[g, :, pl.ds(pl.multiple_of(24 - 24 * xlo, 8), 24), :]
-            next_copy(g, xlo).start()
-            waits.append(next_copy(g, xlo))
+        elif kind == "fs":
+            for dx, dy, dev, value in spread(g):
+                if dev is not None:
+                    g_send[g, dx + 4 * dy] = value().reshape(ROWS * 24, 128).astype(BF16)
+                    give_copy(g, dx + 4 * dy, dev).start()
+                    waits.append(give_copy(g, dx + 4 * dy, dev))
         else:
-            next_copy(g, 1 - xlo).wait_recv()
+            sums = [None, None]
+            for dx, dy, dev, value in spread(g):
+                if dev is None:
+                    v = value().reshape(ROWS * 24, 128)
+                else:
+                    give_copy(g, dx + 4 * dy, dev).wait_recv()
+                    v = g_recv[g, dx + 4 * dy].astype(F32)
+                sums[dx % 2] = v if sums[dx % 2] is None else sums[dx % 2] + v
+            for first, v in zip((base, 12 - base), sums):
+                wg_rows[pl.ds(first + ROWS * g, ROWS)] = (v * scale).reshape(ROWS, 24, 128)
     assert row == 24
     for r in range(24):
         wg_ref[:, r, :] = wg_rows[r]
@@ -437,12 +477,22 @@
         far_copy(p).wait_send()
         for i in range(4):
             core_copy(i, p).wait_send()
-        for i in range(2):
-            x_copy_out(i, p).wait_send()
-        return 0
-
-    lax.fori_loop(0, 6, drain, 0)
+        x_copy_out(0, p).wait_send()
+        return 0
+
+    def drain_x(p, _):
+        x_copy_out(1, p).wait_send()
+        return 0
+
+    def drain_far(p, _):
+        turn_copy(p).wait_send()
+        return 0
+
+    lax.fori_loop(0, PIECES, drain, 0)
+    lax.fori_loop(0, VIA_X, drain_x, 0)
+    lax.fori_loop(VIA_X, PIECES, drain_far, 0)
     x_move.wait_send()
+    dx_copy.wait()
     for stage in stages:
         for ring in stage.values():
             ring.finish()
@@ -453,13 +503,12 @@
 def on_device(features, weights, block_cols, cotangent):
     tok, width = features.shape
     rows = weights.shape[1]
-    row = jnp.arange(rows, dtype=jnp.int32)[:, None, None, None]
-    slot = jnp.arange(12, dtype=jnp.int32)[None, :, None, None]
-    line = jnp.arange(12, dtype=jnp.int32)[None, None, :, None]
-    place = jnp.arange(48, dtype=jnp.int32)[None, None, None, :]
-    cols = block_cols[:, :, None, None]
-    hit = (row // 4 == line % 6) & (jnp.where(line < 6, cols, row % 4 * 12 + slot) == place)
-    meta = jnp.sum(jnp.where(hit, jnp.where(line < 6, row * 12 + slot, cols), 0), axis=(0, 1))
+    row = jnp.arange(rows, dtype=jnp.int32)[:, None, None]
+    slot = jnp.arange(12, dtype=jnp.int32)[None, :, None]
+    place = jnp.arange(24 * rows, dtype=jnp.int32)[None, None, :]
+    cols = block_cols[:, :, None]
+    key = jnp.where(place < 12 * rows, row // 4 * 48 + cols, 12 * rows + row * 12 + slot)
+    meta = jnp.sum(jnp.where(key == place, jnp.where(place < 12 * rows, row * 12 + slot, cols), 0), axis=(0, 1))
     scale = float(tok * lax.axis_size("dp")) ** (-0.5)
     vmem = pl.BlockSpec(memory_space=pltpu.VMEM)
     smem = pl.BlockSpec(memory_space=pltpu.SMEM)
@@ -474,21 +523,22 @@
         functools.partial(kernel, scale),
         out_shape=(jax.ShapeDtypeStruct((tok, width), BF16), jax.ShapeDtypeStruct((24, rows, 128), F32)),
         in_specs=[smem, any_, any_, any_],
-        out_specs=(vmem, vmem),
+        out_specs=(any_, vmem),
         scratch_shapes=[
             pltpu.VMEM((rows * 12, 128, 128), BF16),
             pltpu.VMEM((12, 128, rows, 128), BF16),
             pltpu.VMEM((tok, 1536), BF16),
+            pltpu.VMEM((tok, width), BF16),
             quarter, quarter, quarter, quarter, quarter, quarter,
-            pltpu.VMEM((48, 512, 128), BF16),
+            pltpu.VMEM((48, 256, 128), BF16),
+            pltpu.VMEM((48, 256, 128), BF16),
             pltpu.VMEM((rows, tok, 128), BF16),
             pltpu.VMEM((12, tok, 128), BF16),
             pltpu.VMEM((12, 128, 512), BF16),
             pltpu.VMEM((12, 1536, 128), F32),
             pltpu.VMEM((nz, ROWS, 96, 128), F32),
             pltpu.VMEM((nx, ROWS, 8, 48, 128), F32),
-            pltpu.VMEM((len(UNITS), ROWS * 48, 128), F32),
-            pltpu.VMEM((n_groups, ROWS, 48, 128), F32),
+            pltpu.VMEM((nx, ROWS, 48, 128), F32),
             pltpu.VMEM((rows, 24, 128), F32),
             pltpu.VMEM((nz, 2, ROWS, 96, 128), BF16),
             pltpu.VMEM((nz, 7, ROWS, 96, 128), BF16),
@@ -496,23 +546,18 @@
             pltpu.VMEM((nx, 1, ROWS, 384, 128), BF16),
             pltpu.VMEM((nx, 2, 1, ROWS * 48, 128), BF16),
             pltpu.VMEM((nx, 7, 1, ROWS * 48, 128), BF16),
-            pltpu.VMEM((nz, 1, 1, ROWS * 48, 128), BF16),
-            pltpu.VMEM((nz, 1, 1, ROWS * 48, 128), BF16),
-            pltpu.VMEM((n_groups, ROWS * 48, 128), BF16),
-            pltpu.VMEM((n_groups, ROWS * 48, 128), BF16),
             pltpu.VMEM((ny, ROWS, 768, 128), BF16),
             pltpu.VMEM((ny, ROWS, 768, 128), BF16),
-            pltpu.VMEM((n_groups, ROWS, 24, 128), F32),
-            dma((rows,)), dma((12,)), dma(()),
-            dma((10, 6)), dma((10, 6)),
+            pltpu.VMEM((n_groups, 8, ROWS * 24, 128), BF16),
+            pltpu.VMEM((n_groups, 8, ROWS * 24, 128), BF16),
+            dma((rows,)), dma((12,)), dma(()), dma(()),
+            dma((10, PIECES)), dma((10, PIECES)),
             dma(()), dma(()),
             dma((nz, 7)), dma((nz, 7)),
             dma((nx, 1)), dma((nx, 1)),
             dma((nx, 7)), dma((nx, 7)),
-            dma((nz, 1)), dma((nz, 1)),
-            dma((n_groups,)), dma((n_groups,)),
             dma((ny,)), dma((ny,)),
-            dma((n_groups,)), dma((n_groups,)),
+            dma((n_groups, 8)), dma((n_groups, 8)),
         ],
         compiler_params=pltpu.CompilerParams(
             collective_id=0, has_side_effects=True, vmem_limit_bytes=62 * 2**20),

time: 113 us -> 106 us (0.938)
  Pallas kernels: 106 us -> 99.9 us
    pallas_call x1, Pallas kernels: 106 us -> 99.9 us  [on_device(): pl.pallas_call(functools.partial(kernel, scale), out_shape=(jax.ShapeDtyp...]
where the time goes in v3:
time: 106 us
  Pallas kernels  99.9 us (94%)
  local copies, waits for them, and re-layouts  3.27 us (3%)
  other arithmetic  2.25 us (2%)
    pallas_call x1, Pallas kernels, on_device(): pl.pallas_call(functools.partial(kernel, scale), out_shape=(jax.ShapeDtyp...  99.9 us
    unnamed x4, local copies, waits for them, and re-layouts  3.27 us

profile of v3, /device:TPU:2, one launch (start us, length us, event | category | flops | bytes accessed | tf_op | source)
XLA Modules:
  0.0 106.0 jit_solution(6323175368032801030)
XLA Ops:
  0.7 0.7 broadcast_add_fusion
  1.4 1.5 %select_reduce_fusion.meta_ref = s32[576]{0:T(1024)} fusion(s32[24,12]{0,1:T(8,128)} %param.6, s32[24,12]{0,1:T(8,128)S(1)} %get-tuple-element.2, s32[24,12]{0,1:T(8,128)S(1)} %get-tuple-element.3, s32[24,12]{0,1:T(8,128)S(1)} %broadcast_add_fusion, pred[576]{0:T(1024)(128)(4,1)S(1)} %iota_compare_fusion.1), kind=kLoop, calls=%fused_computation | loop fusion | flops 828864 | bytes 7488 | tf_op jit(solution)/shard_map/reduce_sum | solution.py:511
  2.9 99.9 %block_grads.1 = (bf16[224,3072]{1,0:T(8,128)(2,1)}, f32[24,24,128]{2,1,0:T(8,128)}) custom-call(s32[576]{0:T(1024)} %select_reduce_fusion.meta_ref, bf16[224,3072]{1,0:T(8,128)(2,1)} %x_hbm.1, bf16[1536,24,128]{2,1,0:T(8,128)(2,1)} %w_hbm.1, bf16[224,1536]{1,0:T(8,128)(2,1)} %ct_hbm.1), custom_call_target="tpu_custom_call" | custom-call | tf_op jit(solution)/shard_map/block_grads/pallas_call | solution.py:522
  102.8 0.0 copy-start
  102.8 2.5 %copy.10 = bf16[224,3072]{1,0:T(8,128)(2,1)} copy(bf16[224,3072]{1,0:T(8,128)(2,1)} %get-tuple-element.6) | data formatting | bytes 2752512
  105.3 0.0 copy-done
  105.3 0.7 copy.11
  (5 shorter events, 0.0 us)
Async XLA Ops:
  102.8 2.6 %copy-start = (f32[24,24,128]{2,1,0:T(8,128)S(1)}, f32[24,24,128]{2,1,0:T(8,128)}, u32[]{:S(2)}) copy-start(f32[24,24,128]{2,1,0:T(8,128)} %get-tuple-element.7) | copy-start | bytes 884740

commit v4 on v3

--- a/solution.py
+++ b/solution.py
@@ -498,6 +498,11 @@
             ring.finish()
     for cp in waits:
         cp.wait_send()
+
+
+def hand_on(dx_ref, wg_ref, dx_out, wg_out):
+    dx_out[...] = dx_ref[...]
+    wg_out[...] = wg_ref[...]
 
 
 def on_device(features, weights, block_cols, cotangent):
@@ -563,7 +568,14 @@
             collective_id=0, has_side_effects=True, vmem_limit_bytes=62 * 2**20),
         name="block_grads",
     )(meta, features, weights, cotangent)
-    return dx, wg
+    return pl.pallas_call(
+        hand_on,
+        out_shape=(jax.ShapeDtypeStruct((tok, width), BF16), jax.ShapeDtypeStruct((24, rows, 128), F32)),
+        in_specs=[vmem, vmem],
+        out_specs=(vmem, vmem),
+
+        name="hand_on",
+    )(dx, wg)
 
 
 def solution(mesh):

time: 106 us -> 106 us (level)
  local copies, waits for them, and re-layouts: 3.27 us -> 0 us
  Pallas kernels: 99.9 us -> 102 us
    unnamed x4 -> x0, local copies, waits for them, and re-layouts: 3.27 us -> none
    pallas_call x0 -> x1, Pallas kernels: none -> 2.63 us  [on_device(): pl.pallas_call(hand_on, out_shape=(jax.ShapeDtypeStruct((tok, width), BF1...]
where the time goes in v4:
time: 106 us; the launch traced here: 105 us
  Pallas kernels  102 us (96%)
  other arithmetic  2.25 us (2%)
    pallas_call x1, Pallas kernels, on_device(): pl.pallas_call(functools.partial(kernel, scale), out_shape=(jax.ShapeDtyp...  99.8 us
    pallas_call x1, Pallas kernels, on_device(): pl.pallas_call(hand_on, out_shape=(jax.ShapeDtypeStruct((tok, width), BF1...  2.63 us

profile of v4, /device:TPU:2, one launch (start us, length us, event | category | flops | bytes accessed | tf_op | source)
XLA Modules:
  0.0 105.4 jit_solution(1537203122939398296)
XLA Ops:
  0.7 0.7 broadcast_add_fusion
  1.4 1.5 %select_reduce_fusion.meta_ref = s32[576]{0:T(1024)} fusion(s32[24,12]{0,1:T(8,128)} %param.6, s32[24,12]{0,1:T(8,128)S(1)} %get-tuple-element.6, s32[24,12]{0,1:T(8,128)S(1)} %get-tuple-element.7, s32[24,12]{0,1:T(8,128)S(1)} %broadcast_add_fusion, pred[576]{0:T(1024)(128)(4,1)S(1)} %iota_compare_fusion.1), kind=kLoop, calls=%fused_computation | loop fusion | flops 828864 | bytes 7488 | tf_op jit(solution)/shard_map/reduce_sum | solution.py:516
  2.9 99.8 %block_grads.1 = (bf16[224,3072]{1,0:T(8,128)(2,1)}, f32[24,24,128]{2,1,0:T(8,128)}) custom-call(s32[576]{0:T(1024)} %select_reduce_fusion.meta_ref, bf16[224,3072]{1,0:T(8,128)(2,1)} %x_hbm.1, bf16[1536,24,128]{2,1,0:T(8,128)(2,1)} %w_hbm.1, bf16[224,1536]{1,0:T(8,128)(2,1)} %ct_hbm.1), custom_call_target="tpu_custom_call" | custom-call | tf_op jit(solution)/shard_map/block_grads/pallas_call | solution.py:527
  102.8 2.6 %hand_on.1 = (bf16[224,3072]{1,0:T(8,128)(2,1)}, f32[24,24,128]{2,1,0:T(8,128)}) custom-call(bf16[224,3072]{1,0:T(8,128)(2,1)} %get-tuple-element.4.dx_ref, f32[24,24,128]{2,1,0:T(8,128)} %get-tuple-element.5.wg_ref), custom_call_target="tpu_custom_call" | custom-call | tf_op jit(solution)/shard_map/hand_on/pallas_call | solution.py:571
  (5 shorter events, 0.0 us)
